TPU v7x, 128 devices: a whole 4x4x4 slice. The times are simulated.
128 devices in a mesh: seq: 32 (over z, y, core), batch: 4 (over x).
Axes of the slice: x: 4, y: 4, z: 4, core: 2. Of those that a mesh axis runs over, the one named last changes fastest.
Arguments:
- queries: bfloat16 [65536, 2048], P(('batch', 'seq')), parts along dimension 0, may hold values from -6 to 6
- keys: bfloat16 [65536, 2048], P(('batch', 'seq')), parts along dimension 0, may hold values from -0.5 to 0.5
- values: bfloat16 [65536, 2048], P(('batch', 'seq')), parts along dimension 0, may hold values from -6 to 6
- log_gate: float32 [65536, 2048], P(('batch', 'seq')), parts along dimension 0, may hold values from -1 to 0, as said below
Outputs:
- attended: bfloat16 [65536, 2048], P(('batch', 'seq')), parts along dimension 0
There are 4 independent parts, one for each index of `batch`. A program takes and returns all parts, laid end to end along the dimension named above; each array names one. Nothing has to cross between parts.
Inputs may be any that keep to these rules, and one draw needn't show every extreme that they name: `log_gate`: log-decays of the forget gate per token and key channel; within each aligned block of 128 tokens the log-decays of one key channel sum to at least -40.
All inputs are finite; a program needn't handle non-finite values.
Results may differ from a plain program's by a relative error of at most 0.0063.
Values sent between devices are 32-bit elements; how exact they have to be, the bound alone decides.
No kernel may reach another device: no remote copies, remote signals or barrier semaphores. Data moves between devices by JAX's collectives and lax.ppermute only.
A program may use at most 128 MiB of HBM per device.

v0:
```python
import jax
import jax.numpy as jnp
from jax import lax
from jax.sharding import PartitionSpec as P

H = 16
DK = 128
DV = 128
GROUP = 128


def owners_prefix(flat_state, flat_total):
    devices = lax.axis_size("seq")
    received = (
        lax.all_to_all(flat_state, "seq", split_axis=0, concat_axis=0, tiled=True),
        lax.all_to_all(flat_total, "seq", split_axis=0, concat_axis=0, tiled=True),
    )
    states = received[0].reshape(devices, -1, DV)
    totals = received[1].reshape(devices, -1)
    inclusive = jnp.cumsum(totals, axis=0)
    exclusive = inclusive - totals
    device_order = jnp.arange(devices)
    earlier_mask = (device_order[None, :] < device_order[:, None])[..., None]
    exponent = exclusive[:, None, :] - inclusive[None, :, :]
    weights = jnp.where(earlier_mask, jnp.exp(jnp.where(earlier_mask, exponent, 0.0)), 0.0)
    prefix = jnp.einsum("dsr,srv->drv", weights, states, precision=lax.Precision.HIGHEST)
    return lax.all_to_all(prefix.reshape(-1, DV), "seq", split_axis=0, concat_axis=0, tiled=True)


def on_device(queries, keys, values, log_gate):
    tok_rows = queries.shape[0]
    groups = tok_rows // GROUP
    gate_logs = log_gate.reshape(groups, GROUP, H, DK)
    cumulative = jnp.cumsum(gate_logs, axis=1)
    totals = cumulative[:, -1]
    query_blocks = queries.reshape(groups, GROUP, H, DK).astype(jnp.float32)
    key_blocks = keys.reshape(groups, GROUP, H, DK).astype(jnp.float32)
    value_blocks = values.reshape(groups, GROUP, H, DV)
    query_scaled = (query_blocks * DK ** (-0.5) * jnp.exp(cumulative)).astype(jnp.bfloat16)
    key_inverse = (key_blocks * jnp.exp(-cumulative)).astype(jnp.bfloat16)
    key_to_end = (key_blocks * jnp.exp(totals[:, None] - cumulative)).astype(jnp.bfloat16)
    causal = jnp.arange(GROUP)[:, None] >= jnp.arange(GROUP)[None, :]
    scores = jnp.einsum(
        "nthc,nshc->nhts", query_scaled, key_inverse, preferred_element_type=jnp.float32
    )
    scores = jnp.where(causal[None, None], scores, 0.0).astype(jnp.bfloat16)
    within = jnp.einsum("nhts,nshv->nthv", scores, value_blocks, preferred_element_type=jnp.float32)
    updates = jnp.einsum(
        "nshc,nshv->nhcv", key_to_end, value_blocks, preferred_element_type=jnp.float32
    )

    def advance(carried, inputs):
        update_here, total_here = inputs
        return (jnp.exp(total_here)[..., None] * carried + update_here, carried)

    ending, starts = lax.scan(advance, jnp.zeros((H, DK, DV), jnp.float32), (updates, totals))
    before = jnp.cumsum(totals, axis=0) - totals
    flat_state = ending.reshape(H * DK, DV)
    flat_total = jnp.sum(totals, axis=0).reshape(H * DK)
    prefix = owners_prefix(flat_state, flat_total)
    entry_states = starts + jnp.exp(before)[..., None] * prefix.reshape(H, DK, DV)[None]
    across = jnp.einsum(
        "nthc,nhcv->nthv",
        query_scaled,
        entry_states.astype(jnp.bfloat16),
        preferred_element_type=jnp.float32,
    )
    return (within + across).astype(jnp.bfloat16).reshape(tok_rows, H * DV)


def solution(mesh):
    in_specs = (
        P(("batch", "seq"), None),
        P(("batch", "seq"), None),
        P(("batch", "seq"), None),
        P(("batch", "seq"), None),
    )
    out_specs = P(("batch", "seq"), None)
    return jax.shard_map(
        on_device, mesh=mesh, in_specs=in_specs, out_specs=out_specs, check_vma=False
    )
```

profile of v0, /device:TPU:1, one launch (start us, length us, event | category | flops | bytes accessed | tf_op | source)
XLA Modules:
  0.0 105.0 jit_solution(13191661461280259409)
XLA Ops:
  0.0 3.1 %copy.40 = f32[64,8,16,128]{3,2,1,0:T(8,128)S(1)} copy(f32[64,8,16,128]{3,1,2,0:T(8,128)} %bitcast.68) | data formatting | bytes 8388608
  3.1 0.3 fusion.2
  3.4 0.0 copy-start
  3.4 1.9 %copy-done = f32[4,128,16,128]{3,2,1,0:T(8,128)} copy-done((f32[4,128,16,128]{3,2,1,0:T(8,128)}, f32[4,128,16,128]{3,2,1,0:T(8,128)S(1)}, u32[]{:S(2)}) %copy-start) | copy-done | bytes 4194328
  5.3 0.0 copy-start.3
  5.4 0.7 all_to_all.18
  6.0 9.6 %all-to-all-start.1 = ((f32[32,64,1]{1,2,0:T(1,128)}), f32[32,64,1]{1,2,0:T(1,128)S(1)}, u32[]{:S(2)}, u32[]{:S(2)}) async-start(f32[32,64,1]{1,2,0:T(1,128)} %all_to_all.18), calls=%async_computation.1 | async-start | bytes 32768 | tf_op jit(solution)/shard_map/all_to_all | solution.py:16
  15.7 2.2 %copy.42 = bf16[64,8,16,128]{3,2,1,0:T(8,128)(2,1)S(1)} copy(bf16[64,8,16,128]{3,1,2,0:T(8,128)(2,1)} %bitcast.70) | data formatting | bytes 4194304
  17.9 0.0 copy-done.3
  17.9 0.0 copy-start.2
  17.9 0.6 multiply_bitcast_fusion
  18.5 0.0 copy-start.4
  18.5 0.9 copy.39
  19.4 0.8 copy-done.4
  20.2 0.5 convert_bitcast_fusion
  20.7 0.0 copy-start.1
  20.7 0.9 copy.41
  21.7 1.2 %copy-done.1 = f32[4,128,16,128]{3,2,1,0:T(8,128)S(1)} copy-done((f32[4,128,16,128]{3,2,1,0:T(8,128)S(1)}, f32[4,128,16,128]{3,2,1,0:T(8,128)}, u32[]{:S(2)}) %copy-start.1) | copy-done | bytes 4194328
  22.9 2.8 %fusion.1 = (bf16[4,128,16,128]{3,2,1,0:T(8,128)(2,1)S(1)}, bf16[4,128,16,128]{3,2,1,0:T(8,128)(2,1)}, bf16[4,128,16,128]{3,2,1,0:T(8,128)(2,1)S(1)}) fusion(f32[4,128,16,128]{3,2,1,0:T(8,128)S(1)} %copy-done.1, f32[4,16,128]{2,1,0:T(8,128)S(1)} %get-tuple-element.115, f32[4,128,16,128]{3,2,1,0:T(8,128)S(1)} %bitcast.64, f32[4,128,16,128]{3,2,1,0:T(8,128)S(1)} %bitcast.63), kind=kLoop, calls=%fused_computation.6 | loop fusion | flops 8388608 | bytes 18907136 | tf_op jit(solution)/shard_map/convert_element_type | solution.py:41
  25.7 0.0 copy-done.2
  25.7 2.9 %fusion.6 = f32[4,16,128,128]{3,2,1,0:T(8,128)} fusion(bf16[4,128,16,128]{3,2,1,0:T(8,128)(2,1)S(1)} %get-tuple-element.63, bf16[4,128,16,128]{3,2,1,0:T(8,128)(2,1)S(1)} %bitcast.66), kind=kOutput, calls=%fused_computation.18 | convolution fusion | flops 268435456 | bytes 8388608 | tf_op jit(solution)/shard_map/nshc,nshv->nhcv/dot_general | solution.py:48
  28.6 19.3 %while.14 = (s32[]{:T(128)}, f32[16,128,128]{2,1,0:T(8,128)}, f32[4,16,128,128]{3,2,1,0:T(8,128)}, f32[4,16,128]{2,1,0:T(8,128)S(1)}, f32[4,16,128,128]{3,2,1,0:T(8,128)}) while((s32[]{:T(128)}, f32[16,128,128]{2,1,0:T(8,128)}, f32[4,16,128,128]{3,2,1,0:T(8,128)}, f32[4,16,128]{2,1,0:T(8,128)S(1)}, ...), condition=%wide.region_2.3_spmd.clone.clone, body=%wide.region_1.2_spmd.clone.sunk.clone | while | flops 1048579 | bytes 5267548 | solution.py:56
  28.6 1.2 %bitcast_dynamic-update-slice_fusion.3 = f32[4,16,128,128]{3,2,1,0:T(8,128)} fusion(f32[4,16,128,128]{3,2,1,0:T(8,128)} %get-tuple-element.119, s32[]{:T(128)S(6)} %copy.68, f32[16,128,128]{2,1,0:T(8,128)} %get-tuple-element.118, pred[]{:T(512)S(6)} %compare.4), kind=kLoop, calls=%fused_computation.clone.1.clone | loop fusion | flops 262144 | bytes 2097157 | tf_op jit(solution)/shard_map/while/body/jit(dynamic_update_index_in_dim)/dynamic_update_slice | solution.py:56
  29.8 2.6 %bitcast_add_fusion.4 = f32[16,128,128]{2,1,0:T(8,128)} fusion(f32[4,16,128,128]{3,2,1,0:T(8,128)} %get-tuple-element.126, s32[]{:T(128)S(6)} %copy.68, f32[16,128,128]{2,1,0:T(8,128)} %get-tuple-element.118, f32[16,128]{1,0:T(8,128)S(1)} %exponential_bitcast_fusion.3, pred[]{:T(512)S(6)} %compare.4), kind=kLoop, calls=%fused_computation.1.clone.1.clone | loop fusion | flops 786432 | bytes 3153925 | tf_op jit(solution)/shard_map/while/body/eval_jaxpr/add | solution.py:54
  32.4 2.3 %bitcast_dynamic-update-slice_fusion.3 = f32[4,16,128,128]{3,2,1,0:T(8,128)} fusion(f32[4,16,128,128]{3,2,1,0:T(8,128)} %get-tuple-element.119, s32[]{:T(128)S(6)} %copy.68, f32[16,128,128]{2,1,0:T(8,128)} %get-tuple-element.118, pred[]{:T(512)S(6)} %compare.4), kind=kLoop, calls=%fused_computation.clone.1.clone | loop fusion | flops 262144 | bytes 2097157 | tf_op jit(solution)/shard_map/while/body/jit(dynamic_update_index_in_dim)/dynamic_update_slice | solution.py:56
  34.6 2.9 %bitcast_add_fusion.4 = f32[16,128,128]{2,1,0:T(8,128)} fusion(f32[4,16,128,128]{3,2,1,0:T(8,128)} %get-tuple-element.126, s32[]{:T(128)S(6)} %copy.68, f32[16,128,128]{2,1,0:T(8,128)} %get-tuple-element.118, f32[16,128]{1,0:T(8,128)S(1)} %exponential_bitcast_fusion.3, pred[]{:T(512)S(6)} %compare.4), kind=kLoop, calls=%fused_computation.1.clone.1.clone | loop fusion | flops 786432 | bytes 3153925 | tf_op jit(solution)/shard_map/while/body/eval_jaxpr/add | solution.py:54
  37.5 2.3 %bitcast_dynamic-update-slice_fusion.3 = f32[4,16,128,128]{3,2,1,0:T(8,128)} fusion(f32[4,16,128,128]{3,2,1,0:T(8,128)} %get-tuple-element.119, s32[]{:T(128)S(6)} %copy.68, f32[16,128,128]{2,1,0:T(8,128)} %get-tuple-element.118, pred[]{:T(512)S(6)} %compare.4), kind=kLoop, calls=%fused_computation.clone.1.clone | loop fusion | flops 262144 | bytes 2097157 | tf_op jit(solution)/shard_map/while/body/jit(dynamic_update_index_in_dim)/dynamic_update_slice | solution.py:56
  39.9 2.9 %bitcast_add_fusion.4 = f32[16,128,128]{2,1,0:T(8,128)} fusion(f32[4,16,128,128]{3,2,1,0:T(8,128)} %get-tuple-element.126, s32[]{:T(128)S(6)} %copy.68, f32[16,128,128]{2,1,0:T(8,128)} %get-tuple-element.118, f32[16,128]{1,0:T(8,128)S(1)} %exponential_bitcast_fusion.3, pred[]{:T(512)S(6)} %compare.4), kind=kLoop, calls=%fused_computation.1.clone.1.clone | loop fusion | flops 786432 | bytes 3153925 | tf_op jit(solution)/shard_map/while/body/eval_jaxpr/add | solution.py:54
  42.8 2.3 %bitcast_dynamic-update-slice_fusion.3 = f32[4,16,128,128]{3,2,1,0:T(8,128)} fusion(f32[4,16,128,128]{3,2,1,0:T(8,128)} %get-tuple-element.119, s32[]{:T(128)S(6)} %copy.68, f32[16,128,128]{2,1,0:T(8,128)} %get-tuple-element.118, pred[]{:T(512)S(6)} %compare.4), kind=kLoop, calls=%fused_computation.clone.1.clone | loop fusion | flops 262144 | bytes 2097157 | tf_op jit(solution)/shard_map/while/body/jit(dynamic_update_index_in_dim)/dynamic_update_slice | solution.py:56
  45.1 2.9 %bitcast_add_fusion.4 = f32[16,128,128]{2,1,0:T(8,128)} fusion(f32[4,16,128,128]{3,2,1,0:T(8,128)} %get-tuple-element.126, s32[]{:T(128)S(6)} %copy.68, f32[16,128,128]{2,1,0:T(8,128)} %get-tuple-element.118, f32[16,128]{1,0:T(8,128)S(1)} %exponential_bitcast_fusion.3, pred[]{:T(512)S(6)} %compare.4), kind=kLoop, calls=%fused_computation.1.clone.1.clone | loop fusion | flops 786432 | bytes 3153925 | tf_op jit(solution)/shard_map/while/body/eval_jaxpr/add | solution.py:54
  47.9 0.0 all-to-all-done.1
  48.0 7.4 %all-to-all-start = ((f32[32,64,128]{2,1,0:T(8,128)}), f32[32,64,128]{2,1,0:T(8,128)S(1)}, u32[]{:S(2)}, u32[]{:S(2)}) async-start(f32[32,64,128]{2,1,0:T(8,128)} %bitcast.2), calls=%async_computation | async-start | bytes 2097152 | tf_op jit(solution)/shard_map/all_to_all | solution.py:15
  55.4 0.1 reduce_window_sum.35
  55.4 0.1 copy.30
  55.5 0.1 copy.29
  55.6 16.9 %all-to-all-done = f32[32,64,128]{2,1,0:T(8,128)S(1)} async-done(((f32[32,64,128]{2,1,0:T(8,128)}), f32[32,64,128]{2,1,0:T(8,128)S(1)}, u32[]{:S(2)}, u32[]{:S(2)}) %all-to-all-start) | async-done | bytes 1048608 | tf_op jit(solution)/shard_map/all_to_all | solution.py:15
  72.5 1.8 %convolution_bitcast_fusion = f32[32,64,128]{2,0,1:T(8,128)S(1)} fusion(f32[32,64,128]{2,1,0:T(8,128)S(1)} %all-to-all-done, f32[32,64]{0,1:T(8,128)S(1)} %copy.30, f32[32,64]{0,1:T(8,128)S(1)} %copy.29, pred[32,32]{1,0:T(8,128)(4,1)S(1)} %iota_compare_fusion.1), kind=kOutput, calls=%fused_computation.28 | convolution fusion | flops 100859904 | bytes 2114560 | tf_op jit(solution)/shard_map/dsr,srv->drv/dot_general | solution.py:26
  74.3 1.6 %copy.32 = f32[32,64,128]{2,1,0:T(8,128)} copy(f32[32,64,128]{2,0,1:T(8,128)S(1)} %convolution_bitcast_fusion) | data formatting | bytes 2097152 | tf_op jit(solution)/shard_map/dsr,srv->drv/transpose | solution.py:26
  75.9 4.0 %all-to-all-start.2 = ((f32[32,64,128]{2,1,0:T(8,128)}), f32[32,64,128]{2,1,0:T(8,128)S(1)}, u32[]{:S(2)}, u32[]{:S(2)}) async-start(f32[32,64,128]{2,1,0:T(8,128)} %copy.32), calls=%async_computation.2 | async-start | bytes 2097152 | tf_op jit(solution)/shard_map/all_to_all | solution.py:27
  79.9 1.0 fusion.20
  80.9 6.4 %fusion.12 = f32[4,16,128,128]{3,2,1,0:T(8,128)} fusion(bf16[4,128,16,128]{3,2,1,0:T(8,128)(2,1)} %bitcast.67, bf16[4,128,16,128]{3,2,1,0:T(8,128)(2,1)} %get-tuple-element.64, pred[128,128]{1,0:T(8,128)(4,1)S(1)} %iota_compare_fusion, bf16[4,128,16,128]{3,2,1,0:T(8,128)(2,1)S(1)} %get-tuple-element.67), kind=kOutput, calls=%fused_computation.24 | convolution fusion | flops 538968064 | bytes 10502144 | tf_op jit(solution)/shard_map/nhts,nshv->nthv/dot_general | solution.py:47
  87.3 9.8 %all-to-all-done.2 = f32[32,64,128]{2,1,0:T(8,128)S(1)} async-done(((f32[32,64,128]{2,1,0:T(8,128)}), f32[32,64,128]{2,1,0:T(8,128)S(1)}, u32[]{:S(2)}, u32[]{:S(2)}) %all-to-all-start.2) | async-done | bytes 1048608 | tf_op jit(solution)/shard_map/all_to_all | solution.py:27
  97.2 4.6 %fusion.5 = bf16[4,128,16,128]{3,1,2,0:T(8,128)(2,1)S(1)} fusion(f32[4,16,128,128]{3,2,1,0:T(8,128)} %fusion.12, f32[4,16,128,128]{3,2,1,0:T(8,128)} %get-tuple-element.33, f32[16,128,128]{2,1,0:T(8,128)S(1)} %bitcast.69, f32[4,16,128]{2,1,0:T(8,128)S(1)} %fusion.20, bf16[4,128,16,128]{3,2,1,0:T(8,128)(2,1)S(1)} %get-tuple-element.67), kind=kOutput, calls=%fused_computation.12 | convolution fusion | flops 273678336 | bytes 13664256 | tf_op jit(solution)/shard_map/nthc,nhcv->nthv/dot_general | solution.py:62
  101.8 1.4 %copy.36 = bf16[4,128,16,128]{3,2,1,0:T(8,128)(2,1)S(1)} copy(bf16[4,128,16,128]{3,1,2,0:T(8,128)(2,1)S(1)} %fusion.5) | data formatting | bytes 4194304 | tf_op jit(solution)/shard_map/convert_element_type | solution.py:68
  103.1 1.9 %copy.63 = bf16[64,8,16,128]{3,1,2,0:T(8,128)(2,1)} copy(bf16[64,8,16,128]{3,2,1,0:T(8,128)(2,1)S(1)} %bitcast.65) | data formatting | bytes 4194304
  (10 shorter events, 0.1 us)
Async XLA Ops:
  3.4 1.9 %copy-start = (f32[4,128,16,128]{3,2,1,0:T(8,128)}, f32[4,128,16,128]{3,2,1,0:T(8,128)S(1)}, u32[]{:S(2)}) copy-start(f32[4,128,16,128]{3,2,1,0:T(8,128)S(1)} %fusion.2) | copy-start | bytes 12582916
  5.3 12.5 %copy-start.3 = (bf16[512,2048]{1,0:T(8,128)(2,1)S(1)}, bf16[512,2048]{1,0:T(8,128)(2,1)}, u32[]{:S(2)}) copy-start(bf16[512,2048]{1,0:T(8,128)(2,1)} %param.6) | copy-start | bytes 6291460
  6.0 41.9 %all-to-all-start.1 = ((f32[32,64,1]{1,2,0:T(1,128)}), f32[32,64,1]{1,2,0:T(1,128)S(1)}, u32[]{:S(2)}, u32[]{:S(2)}) async-start(f32[32,64,1]{1,2,0:T(1,128)} %all_to_all.18), calls=%async_computation.1 | async-start | bytes 32768 | tf_op jit(solution)/shard_map/all_to_all | solution.py:16
  17.9 7.8 %copy-start.2 = (bf16[64,8,16,128]{3,2,1,0:T(8,128)(2,1)}, bf16[64,8,16,128]{3,2,1,0:T(8,128)(2,1)S(1)}, u32[]{:S(2)}) copy-start(bf16[64,8,16,128]{3,2,1,0:T(8,128)(2,1)S(1)} %copy.42) | copy-start | bytes 6291460
  18.5 1.7 %copy-start.4 = (bf16[512,2048]{1,0:T(8,128)(2,1)S(1)}, bf16[512,2048]{1,0:T(8,128)(2,1)}, u32[]{:S(2)}) copy-start(bf16[512,2048]{1,0:T(8,128)(2,1)} %param.7) | copy-start | bytes 6291460
  20.7 2.2 %copy-start.1 = (f32[4,128,16,128]{3,2,1,0:T(8,128)S(1)}, f32[4,128,16,128]{3,2,1,0:T(8,128)}, u32[]{:S(2)}) copy-start(f32[4,128,16,128]{3,2,1,0:T(8,128)} %copy-done) | copy-start | bytes 12582916
  48.0 24.6 %all-to-all-start = ((f32[32,64,128]{2,1,0:T(8,128)}), f32[32,64,128]{2,1,0:T(8,128)S(1)}, u32[]{:S(2)}, u32[]{:S(2)}) async-start(f32[32,64,128]{2,1,0:T(8,128)} %bitcast.2), calls=%async_computation | async-start | bytes 2097152 | tf_op jit(solution)/shard_map/all_to_all | solution.py:15
  75.9 21.3 %all-to-all-start.2 = ((f32[32,64,128]{2,1,0:T(8,128)}), f32[32,64,128]{2,1,0:T(8,128)S(1)}, u32[]{:S(2)}, u32[]{:S(2)}) async-start(f32[32,64,128]{2,1,0:T(8,128)} %copy.32), calls=%async_computation.2 | async-start | bytes 2097152 | tf_op jit(solution)/shard_map/all_to_all | solution.py:27
where the time goes:
time: 106 us; the launch traced here: 105 us
  waiting for transfers between devices  26.8 us (25%)
  other arithmetic  24.5 us (23%)
  starting transfers between devices  21 us (20%)
  local copies, waits for them, and re-layouts  16.8 us (16%)
  matrix products  15.7 us (15%)
    all_to_all x1, waiting for transfers between devices, owners_prefix(): lax.all_to_all(flat_state, 'seq', split_axis=0, concat_axis=0, tiled=True)  16.9 us
    unnamed x15, local copies, waits for them, and re-layouts  13 us
    add x4, other arithmetic, advance(): return (jnp.exp(total_here)[..., None] * carried + update_here, carried)  11.3 us
    all_to_all x1, waiting for transfers between devices, owners_prefix(): lax.all_to_all(prefix.reshape(-1, DV), 'seq', split_axis=0, concat_axis=0...  9.84 us
    all_to_all x1, starting transfers between devices, owners_prefix(): lax.all_to_all(flat_total, 'seq', split_axis=0, concat_axis=0, tiled=True)  9.6 us
    dynamic_update_slice x4, other arithmetic, on_device(): lax.scan(advance, jnp.zeros((H, DK, DV), jnp.float32), (updates, totals))  8.06 us
    all_to_all x1, starting transfers between devices, owners_prefix(): lax.all_to_all(flat_state, 'seq', split_axis=0, concat_axis=0, tiled=True)  7.38 us
    dot_general x1, matrix products, on_device(): jnp.einsum('nhts,nshv->nthv', scores, value_blocks, preferred_element_typ...  6.44 us
  transfers between devices with their start and end apart: 3, of which 2 were waited for; matrix products, arithmetic and copies ran while one was open for 36% of the time, Pallas kernels for 0%

commit v1 on v0

v1 whole, which is shorter than its diff:
```python
import functools
import math

import jax
import jax.numpy as jnp
from jax import lax
from jax.experimental import pallas as pl
from jax.experimental.pallas import tpu as pltpu
from jax.sharding import PartitionSpec as P

H = 16
DK = 128
DV = 128
GROUP = 128
HALF = H // 2
WIDTH = HALF * DK
HEADS_STEP = 2
LANES = HEADS_STEP * DK
STEPS = HALF // HEADS_STEP
EARLY = 2
CHUNKS = 4
ROWS = 64
SLICE = ROWS + 8
LOG2E = math.log2(math.e)
LOG2_SCALE = -0.5 * math.log2(DK)

NT = (((1,), (1,)), ((), ()))
TN = (((0,), (0,)), ((), ()))

VMEM = pl.BlockSpec(memory_space=pltpu.VMEM)
SMEM = pl.BlockSpec(memory_space=pltpu.SMEM)
HBM = pl.BlockSpec(memory_space=pltpu.HBM)
ANY = pl.BlockSpec(memory_space=pl.ANY)


def in_vmem(x):
    return pltpu.with_memory_space_constraint(x, pltpu.VMEM)


def in_hbm(x):
    return pltpu.with_memory_space_constraint(x, pltpu.HBM)


def dot(a, b, dims=(((1,), (0,)), ((), ()))):
    return lax.dot_general(a, b, dims, preferred_element_type=jnp.float32)


def triangle(strict_upper):
    row = lax.broadcasted_iota(jnp.int32, (GROUP, 2 * GROUP), 0)
    col = lax.broadcasted_iota(jnp.int32, (GROUP, 2 * GROUP), 1)
    col = jnp.where(col >= GROUP, col - GROUP, col)
    keep = col > row if strict_upper else col <= row
    return jnp.where(keep, 1.0, 0.0).astype(jnp.bfloat16)


def partial_sums(ones, gate):
    high = gate.astype(jnp.bfloat16)
    low = (gate - high.astype(jnp.float32)).astype(jnp.bfloat16)
    return dot(ones, jnp.concatenate([high, low], axis=0))


def columns(half, step):
    return pl.ds(pl.multiple_of(half * WIDTH + step * LANES, LANES), LANES)


def states_step(step, gate_ref, key_ref, value_ref, out_ref):
    ones = triangle(True)
    state = [jnp.zeros((DV, DK), jnp.float32)] * HEADS_STEP
    total = [jnp.zeros((1, DK), jnp.float32)] * HEADS_STEP
    cols = pl.ds(step * LANES, LANES)
    for group in range(gate_ref.shape[0] // GROUP):
        rows = pl.ds(group * GROUP, GROUP)
        gate = gate_ref[rows, cols] * LOG2E
        later = partial_sums(ones, gate)
        gamma = later[0:1] + gate[0:1]
        to_end = (key_ref[rows, cols].astype(jnp.float32) * jnp.exp2(later)).astype(jnp.bfloat16)
        decay = jnp.exp2(gamma)
        for head in range(HEADS_STEP):
            at = slice(head * DK, (head + 1) * DK)
            value = value_ref[rows, pl.ds(step * LANES + head * DV, DV)]
            state[head] = state[head] * decay[:, at] + dot(value, to_end[:, at], TN)
            total[head] = total[head] + gamma[:, at]
    for head in range(HEADS_STEP):
        for part in range(2):
            at = 2 * (step * HEADS_STEP + head) + part
            out_ref[at, 0:ROWS, :] = state[head][ROWS * part : ROWS * (part + 1)]
            out_ref[at, ROWS:SLICE, :] = jnp.broadcast_to(total[head], (SLICE - ROWS, DK))


def column_copies(half, steps, sources, targets, sems):
    copies = []
    for step in steps:
        for source, target in zip(sources, targets):
            at = pl.ds(step * LANES, LANES)
            copies.append(
                pltpu.make_async_copy(source.at[:, columns(half, step)], target.at[:, at], sems.at[len(copies)])
            )
    for copy in copies:
        copy.start()
    return [copies[i : i + len(sources)] for i in range(0, len(copies), len(sources))]


def wait_all(copies):
    for copy in copies:
        copy.wait()


def rest_states_kernel(
    core_ref, gate_hbm, key_hbm, value_hbm, out_ref, own_gate, own_key, own_value, gate, key, value, sems, own_sems
):
    sources = (gate_hbm, key_hbm, value_hbm)
    mine = column_copies(1 - core_ref[0], range(STEPS), sources, (gate, key, value), sems)
    early = column_copies(core_ref[0], range(EARLY), sources, (own_gate, own_key, own_value), own_sems)
    for step in range(STEPS):
        wait_all(mine[step])
        states_step(step, gate, key, value, out_ref)
    for copies in early:
        wait_all(copies)


def rest_states(core, gate, keys, values):
    tokens = keys.shape[0]
    kinds = [x.dtype for x in (gate, keys, values)]
    return pl.pallas_call(
        rest_states_kernel,
        in_specs=[SMEM, HBM, HBM, HBM],
        out_specs=[VMEM] * 4,
        out_shape=[pltpu.VMEM((2 * HALF, SLICE, DK), jnp.float32)]
        + [pltpu.VMEM((tokens, EARLY * LANES), kind) for kind in kinds],
        scratch_shapes=[pltpu.VMEM((tokens, WIDTH), kind) for kind in kinds]
        + [pltpu.SemaphoreType.DMA((3 * STEPS,)), pltpu.SemaphoreType.DMA((3 * EARLY,))],
        compiler_params=pltpu.CompilerParams(vmem_limit_bytes=8 << 20),
        cost_estimate=pl.CostEstimate(flops=10**9, bytes_accessed=9 * 10**6, transcendentals=10**6),
        name="rest_states",
    )(core, in_hbm(gate), in_hbm(keys), in_hbm(values))


def own_states_kernel(
    core_ref, gate_hbm, key_hbm, value_hbm, early_gate, early_key, early_value, out_ref, gate, key, value, sems
):
    mine = column_copies(
        core_ref[0], range(EARLY, STEPS), (gate_hbm, key_hbm, value_hbm), (gate, key, value), sems
    )
    for step in range(EARLY):
        states_step(step, early_gate, early_key, early_value, out_ref)
    for step in range(EARLY, STEPS):
        wait_all(mine[step - EARLY])
        states_step(step, gate, key, value, out_ref)


def own_states(core, gate, keys, values, early):
    tokens = keys.shape[0]
    kinds = [x.dtype for x in (gate, keys, values)]
    return pl.pallas_call(
        own_states_kernel,
        in_specs=[SMEM, HBM, HBM, HBM] + [VMEM] * 3,
        out_specs=VMEM,
        out_shape=pltpu.VMEM((2 * HALF, SLICE, DK), jnp.float32),
        scratch_shapes=[pltpu.VMEM((tokens, WIDTH), kind) for kind in kinds]
        + [pltpu.SemaphoreType.DMA((3 * (STEPS - EARLY),))],
        compiler_params=pltpu.CompilerParams(vmem_limit_bytes=8 << 20),
        cost_estimate=pl.CostEstimate(flops=10**9, bytes_accessed=5 * 10**6, transcendentals=10**6),
        name="own_states",
    )(core, in_hbm(gate), in_hbm(keys), in_hbm(values), *map(in_vmem, early))


def combine_kernel(core_ref, mine_ref, other_ref, out_hbm, other_hbm, out_ref, sems):
    copies = [pltpu.make_async_copy(other_ref, other_hbm, sems.at[CHUNKS])]
    copies[0].start()
    first = core_ref[0] == 0
    length = mine_ref.shape[0] // CHUNKS
    for chunk in range(CHUNKS):
        at = pl.ds(chunk * length, length)
        mine_total = mine_ref[at, ROWS:SLICE, :]
        other_total = other_ref[at, ROWS:SLICE, :]
        mine_weight = jnp.where(first, jnp.exp2(other_total), 1.0)[:, 0:1]
        other_weight = jnp.where(first, 1.0, jnp.exp2(mine_total))[:, 0:1]
        out_ref[at, 0:ROWS, :] = mine_ref[at, 0:ROWS, :] * mine_weight + other_ref[at, 0:ROWS, :] * other_weight
        out_ref[at, ROWS:SLICE, :] = mine_total + other_total
        copies.append(pltpu.make_async_copy(out_ref.at[at], out_hbm.at[at], sems.at[chunk]))
        copies[-1].start()
    wait_all(copies)


def combine(core, mine, other):
    return pl.pallas_call(
        combine_kernel,
        in_specs=[SMEM, VMEM, VMEM],
        out_specs=[HBM, HBM],
        out_shape=[pltpu.HBM(mine.shape, jnp.float32)] * 2,
        scratch_shapes=[pltpu.VMEM(mine.shape, jnp.float32), pltpu.SemaphoreType.DMA((CHUNKS + 1,))],
        compiler_params=pltpu.CompilerParams(vmem_limit_bytes=4 << 20),
        name="combine",
    )(core, in_vmem(mine), in_vmem(other))


def prefix_kernel(in_ref, _, out_hbm, out_ref, sems):
    running = jnp.zeros((ROWS, DK), jnp.float32)
    chips = in_ref.shape[0]
    copies = []
    for chip in range(chips):
        out_ref[chip] = running
        if (chip + 1) % CHUNKS == 0:
            at = pl.ds(chip + 1 - CHUNKS, CHUNKS)
            copies.append(pltpu.make_async_copy(out_ref.at[at], out_hbm.at[at], sems.at[len(copies)]))
            copies[-1].start()
        if chip < chips - 1:
            decay = jnp.exp2(in_ref[chip, ROWS : ROWS + 1, :])
            running = running * decay + in_ref[chip, 0:ROWS, :]
    wait_all(copies)


def prefix(received, after):
    shape = (received.shape[0], ROWS, DK)
    return pl.pallas_call(
        prefix_kernel,
        in_specs=[VMEM, ANY],
        out_specs=HBM,
        out_shape=pltpu.HBM(shape, jnp.float32),
        scratch_shapes=[pltpu.VMEM(shape, jnp.float32), pltpu.SemaphoreType.DMA((shape[0] // CHUNKS,))],
        compiler_params=pltpu.CompilerParams(vmem_limit_bytes=4 << 20),
        name="prefix",
    )(in_vmem(received), after)


def local_step(step, second, query_ref, key_ref, value_ref, gate_ref, init_ref, local_ref, decayed_ref):
    ones = triangle(False)
    row = lax.broadcasted_iota(jnp.int32, (GROUP, GROUP), 0)
    col = lax.broadcasted_iota(jnp.int32, (GROUP, GROUP), 1)
    causal = row >= col
    cols = pl.ds(step * LANES, LANES)
    state, total = [], []
    for head in range(HEADS_STEP):
        at = 2 * (step * HEADS_STEP + head)
        start = jnp.concatenate([init_ref[at, 0:ROWS, :], init_ref[at + 1, 0:ROWS, :]], axis=0)
        state.append(jnp.where(second, start, 0.0))
        total.append(jnp.where(second, init_ref[at, ROWS : ROWS + 1, :], 0.0))
    groups = gate_ref.shape[0] // GROUP
    for group in range(groups):
        rows = pl.ds(group * GROUP, GROUP)
        inclusive = partial_sums(ones, gate_ref[rows, cols] * LOG2E)
        gamma = inclusive[GROUP - 1 : GROUP]
        decay = jnp.exp2(gamma)
        query = query_ref[rows, cols].astype(jnp.float32) * jnp.exp2(inclusive + LOG2_SCALE)
        key = key_ref[rows, cols].astype(jnp.float32) * jnp.exp2(-inclusive)
        query_scaled = query.astype(jnp.bfloat16)
        key_inverse = key.astype(jnp.bfloat16)
        to_end = (key * decay).astype(jnp.bfloat16)
        before = jnp.exp2(jnp.concatenate(total, axis=1))
        decayed_ref[rows, cols] = (query * before).astype(jnp.bfloat16)
        for head in range(HEADS_STEP):
            at = slice(head * DK, (head + 1) * DK)
            head_cols = pl.ds(step * LANES + head * DV, DV)
            value = value_ref[rows, head_cols]
            scores = dot(query_scaled[:, at], key_inverse[:, at], NT)
            scores = jnp.where(causal, scores, 0.0).astype(jnp.bfloat16)
            out = dot(scores, value) + dot(query_scaled[:, at], state[head].astype(jnp.bfloat16), NT)
            local_ref[rows, head_cols] = out.astype(local_ref.dtype)
            if group < groups - 1:
                state[head] = state[head] * decay[:, at] + dot(value, to_end[:, at], TN)
                total[head] = total[head] + gamma[:, at]


def local_kernel(rest, core_ref, query_hbm, key_hbm, value_hbm, gate_hbm, init_any, local_out, decayed_out, done_ref, *refs):
    query, key, value, gate, init, sems, init_sem = refs[:7]
    core = core_ref[0]
    half = 1 - core if rest else core
    fetch = pltpu.make_async_copy(init_any, init, init_sem)
    fetch.start()
    copies = column_copies(
        half, range(STEPS), (gate_hbm, query_hbm, key_hbm, value_hbm), (gate, query, key, value), sems
    )
    fetch.wait()
    local_ref, decayed_ref = refs[7:9] if rest else (local_out, decayed_out)
    stores = []
    for step in range(STEPS):
        wait_all(copies[step])
        local_step(step, core == 1, query, key, value, gate, init, local_ref, decayed_ref)
        if rest:
            at = pl.ds(step * LANES, LANES)
            for ref, out in ((local_ref, local_out), (decayed_ref, decayed_out)):
                stores.append(pltpu.make_async_copy(ref.at[:, at], out.at[:, at], refs[9].at[len(stores)]))
                stores[-1].start()
    wait_all(stores)
    done_ref[...] = jnp.zeros_like(done_ref)


def local_part(rest, core, queries, keys, values, gate, init):
    tokens = keys.shape[0]
    place = pltpu.HBM if rest else pltpu.VMEM
    half = ((tokens, WIDTH), jnp.bfloat16)
    scratch = [pltpu.VMEM((tokens, WIDTH), x.dtype) for x in (queries, keys, values, gate)]
    scratch += [pltpu.VMEM(init.shape, init.dtype), pltpu.SemaphoreType.DMA((4 * STEPS,)), pltpu.SemaphoreType.DMA]
    if rest:
        scratch += [pltpu.VMEM(*half)] * 2 + [pltpu.SemaphoreType.DMA((2 * STEPS,))]
    return pl.pallas_call(
        functools.partial(local_kernel, rest),
        in_specs=[SMEM] + [HBM] * 5,
        out_specs=[HBM if rest else VMEM] * 2 + [VMEM],
        out_shape=[place(*half)] * 2 + [jax.ShapeDtypeStruct((8, DK), jnp.float32)],
        scratch_shapes=scratch,
        compiler_params=pltpu.CompilerParams(vmem_limit_bytes=12 << 20),
        cost_estimate=pl.CostEstimate(flops=4 * 10**9, bytes_accessed=8 * 10**6, transcendentals=10**6),
        name="rest_local" if rest else "own_local",
    )(core, in_hbm(queries), in_hbm(keys), in_hbm(values), in_hbm(gate), in_hbm(init))


def final_step(step, local_ref, decayed_ref, entry_ref, out_ref):
    for head in range(step * HEADS_STEP, (step + 1) * HEADS_STEP):
        at = slice(head * DK, (head + 1) * DK)
        across = dot(decayed_ref[:, at], entry_ref[at, :].astype(jnp.bfloat16), NT)
        out_ref[:, at] = (local_ref[:, at].astype(jnp.float32) + across).astype(jnp.bfloat16)


def final_steps(half, local_ref, decayed_ref, entry_ref, out_hbm, out_ref, sems):
    copies = []
    for step in range(STEPS):
        final_step(step, local_ref, decayed_ref, entry_ref, out_ref)
        at = pl.ds(step * LANES, LANES)
        copies.append(pltpu.make_async_copy(out_ref.at[:, at], out_hbm.at[:, columns(half, step)], sems.at[step]))
        copies[-1].start()
    wait_all(copies)


def own_final_kernel(core_ref, local, decayed, entry, local_hbm, decayed_hbm, _, out_hbm, rest_local, rest_decayed, *refs):
    out_ref, sems, fetch_sems = refs
    fetches = [
        pltpu.make_async_copy(local_hbm, rest_local, fetch_sems.at[0]),
        pltpu.make_async_copy(decayed_hbm, rest_decayed, fetch_sems.at[1]),
    ]
    for fetch in fetches:
        fetch.start()
    final_steps(core_ref[0], local, decayed, entry, out_hbm, out_ref, sems)
    wait_all(fetches)


def own_final(core, local, decayed, entry, rest_local, rest_decayed, after):
    tokens = local.shape[0]
    return pl.pallas_call(
        own_final_kernel,
        in_specs=[SMEM] + [VMEM] * 3 + [HBM] * 2 + [ANY],
        out_specs=[HBM, VMEM, VMEM],
        out_shape=[jax.ShapeDtypeStruct((tokens, H * DV), jnp.bfloat16)]
        + [pltpu.VMEM(x.shape, x.dtype) for x in (rest_local, rest_decayed)],
        scratch_shapes=[
            pltpu.VMEM((tokens, WIDTH), jnp.bfloat16),
            pltpu.SemaphoreType.DMA((STEPS,)),
            pltpu.SemaphoreType.DMA((2,)),
        ],
        compiler_params=pltpu.CompilerParams(vmem_limit_bytes=8 << 20),
        cost_estimate=pl.CostEstimate(flops=10**9, bytes_accessed=4 * 10**6, transcendentals=0),
        name="own_final",
    )(core, *map(in_vmem, (local, decayed, entry)), in_hbm(rest_local), in_hbm(rest_decayed), after)


def rest_final_kernel(core_ref, local, decayed, entry, _, out_hbm, out_ref, sems):
    final_steps(1 - core_ref[0], local, decayed, entry, out_hbm, out_ref, sems)


def rest_final(core, local, decayed, entry, out):
    tokens = local.shape[0]
    return pl.pallas_call(
        rest_final_kernel,
        in_specs=[SMEM] + [VMEM] * 3 + [ANY],
        out_specs=HBM,
        out_shape=jax.ShapeDtypeStruct((tokens, H * DV), jnp.bfloat16),
        input_output_aliases={4: 0},
        scratch_shapes=[pltpu.VMEM((tokens, WIDTH), jnp.bfloat16), pltpu.SemaphoreType.DMA((STEPS,))],
        compiler_params=pltpu.CompilerParams(vmem_limit_bytes=8 << 20),
        cost_estimate=pl.CostEstimate(flops=10**9, bytes_accessed=4 * 10**6, transcendentals=0),
        name="rest_final",
    )(core, *map(in_vmem, (local, decayed, entry)), out)


def on_device(queries, keys, values, log_gate):
    devices = lax.axis_size("seq")
    chips = devices // 2
    core = lax.rem(lax.axis_index("seq"), 2).astype(jnp.int32)[None]
    swap = [(i, i ^ 1) for i in range(devices)]
    same_core = [[2 * chip + c for chip in range(chips)] for c in range(2)]

    def exchange(blocks):
        return lax.all_to_all(blocks, "seq", split_axis=0, concat_axis=0, axis_index_groups=same_core, tiled=True)

    rest, *early = rest_states(core, log_gate, keys, values)
    own_other = lax.ppermute(rest, "seq", swap)
    own = own_states(core, log_gate, keys, values, early)
    rest_other = lax.ppermute(own, "seq", swap)
    combined, own_other = combine(core, own, own_other)
    received = exchange(combined)
    own_local, own_decayed, own_done = local_part(False, core, queries, keys, values, log_gate, own_other)
    own_entry = exchange(prefix(received, own_done))
    rest_local, rest_decayed, rest_done = local_part(True, core, queries, keys, values, log_gate, rest_other)
    own_entry, rest_done = lax.optimization_barrier((own_entry, rest_done))
    own_entry = own_entry.reshape(HALF * DV, DK)
    rest_entry = lax.ppermute(own_entry, "seq", swap)
    out, local, decayed = own_final(core, own_local, own_decayed, own_entry, rest_local, rest_decayed, rest_done)
    return rest_final(core, local, decayed, rest_entry, out)


def solution(mesh):
    spec = P(("batch", "seq"), None)
    return jax.shard_map(on_device, mesh=mesh, in_specs=(spec,) * 4, out_specs=spec, check_vma=False)
```

time: 106 us -> 48.3 us (0.46)
  Pallas kernels: 0 us -> 27.7 us
  other arithmetic: 24.5 us -> 0 us
  waiting for transfers between devices: 26.8 us -> 4.51 us
  local copies, waits for them, and re-layouts: 16.8 us -> 0 us
  matrix products: 15.7 us -> 0 us
  starting transfers between devices: 21 us -> 15.6 us
    pallas_call x0 -> x8, Pallas kernels: none -> 27.7 us  [the longest x2 17.1 us: local_part(): pl.pallas_call(functools.partial(local_kernel, rest), in_specs=[SMEM] + [...]
    all_to_all x3 -> x2, waiting for transfers between devices: 26.8 us -> 4.5 us  [exchange(): lax.all_to_all(blocks, 'seq', split_axis=0, concat_axis=0, axis_index_gro...]
    dot_general x4 -> x0, matrix products: 15.7 us -> none  [the longest x1 6.44 us: on_device(): jnp.einsum('nhts,nshv->nthv', scores, value_blocks, preferred_element_typ...]
    unnamed x15 -> x0, local copies, waits for them, and re-layouts: 13 us -> none
    add x4 -> x0, other arithmetic: 11.3 us -> none  [advance(): return (jnp.exp(total_here)[..., None] * carried + update_here, carried)]
    all_to_all x3 -> x2, starting transfers between devices: 21 us -> 11.4 us  [exchange(): lax.all_to_all(blocks, 'seq', split_axis=0, concat_axis=0, axis_index_gro...]
    dynamic_update_slice x4 -> x0, other arithmetic: 8.06 us -> none  [on_device(): lax.scan(advance, jnp.zeros((H, DK, DV), jnp.float32), (updates, totals))]
    ppermute x0 -> x3, starting transfers between devices: none -> 4.16 us  [the longest x1 2.28 us: on_device(): rest_entry = lax.ppermute(own_entry, 'seq', swap)]
  transfers between devices with their start and end apart: 3 -> 5, of which waited for: 2 -> 2; matrix products, arithmetic and copies ran while one was open for 36% -> 0% of each run, Pallas kernels for 0% -> 46%
where the time goes in v1:
time: 48.3 us; the launch traced here: 48 us
  Pallas kernels  27.7 us (57%)
  starting transfers between devices  15.6 us (32%)
  waiting for transfers between devices  4.51 us (9%)
    pallas_call x2, Pallas kernels, local_part(): pl.pallas_call(functools.partial(local_kernel, rest), in_specs=[SMEM] + [...  17.1 us
    all_to_all x2, starting transfers between devices, exchange(): lax.all_to_all(blocks, 'seq', split_axis=0, concat_axis=0, axis_index_gro...  11.4 us
    all_to_all x2, waiting for transfers between devices, exchange(): lax.all_to_all(blocks, 'seq', split_axis=0, concat_axis=0, axis_index_gro...  4.5 us
    pallas_call x1, Pallas kernels, rest_states(): pl.pallas_call(rest_states_kernel, in_specs=[SMEM, HBM, HBM, HBM], out_sp...  3.35 us
    ppermute x1, starting transfers between devices, on_device(): rest_entry = lax.ppermute(own_entry, 'seq', swap)  2.28 us
    pallas_call x1, Pallas kernels, own_states(): pl.pallas_call(own_states_kernel, in_specs=[SMEM, HBM, HBM, HBM] + [VMEM]...  2.2 us
    pallas_call x1, Pallas kernels, own_final(): pl.pallas_call(own_final_kernel, in_specs=[SMEM] + [VMEM] * 3 + [HBM] * 2...  2.01 us
    ppermute x1, starting transfers between devices, on_device(): own_other = lax.ppermute(rest, 'seq', swap)  1.5 us
  transfers between devices with their start and end apart: 5, of which 2 were waited for; matrix products, arithmetic and copies ran while one was open for 0% of the time, Pallas kernels for 46%

profile of v1, /device:TPU:1, one launch (start us, length us, event | category | flops | bytes accessed | tf_op | source)
XLA Modules:
  0.0 48.0 jit_solution(10456746080409554522)
XLA Ops:
  0.0 3.4 %rest_states.1 = (f32[16,72,128]{2,1,0:T(8,128)S(1)}, f32[512,512]{1,0:T(8,128)S(1)}, bf16[512,512]{1,0:T(8,128)(2,1)S(1)}, bf16[512,512]{1,0:T(8,128)(2,1)S(1)}) custom-call(s32[1]{0:T(128)} %bitcast.core_ref, f32[512,2048]{1,0:T(8,128)} %gate_hbm.7, bf16[512,2048]{1,0:T(8,128)(2,1)} %key_hbm.7, bf16[512,2048]{1,0:T(8,128)(2,1)} %value_hbm.7), custom_call_target="tpu_custom_call" | custom-call | flops 1000000000 | bytes 9000000 | tf_op jit(solution)/shard_map/rest_states/pallas_call | solution.py:124
  3.4 1.5 %collective-permute-start = (f32[16,72,128]{2,1,0:T(8,128)S(1)}, f32[16,72,128]{2,1,0:T(8,128)S(1)}, u32[]{:S(2)}, u32[]{:S(2)}) collective-permute-start(f32[16,72,128]{2,1,0:T(8,128)S(1)} %get-tuple-element.25), channel_id=1, source_target_pairs={{0,4},{4,0},{8,12},{12,8},{16,20},{20,16},{24,28},{28,24},{32,36},... | collective-permute-start | bytes 1769480 | tf_op jit(solution)/shard_map/ppermute | solution.py:386
  4.9 2.2 %own_states.1.mine_ref = f32[16,72,128]{2,1,0:T(8,128)S(1)} custom-call(s32[1]{0:T(128)} %bitcast.core_ref, f32[512,2048]{1,0:T(8,128)} %gate_hbm.7, bf16[512,2048]{1,0:T(8,128)(2,1)} %key_hbm.7, bf16[512,2048]{1,0:T(8,128)(2,1)} %value_hbm.7, f32[512,512]{1,0:T(8,128)S(1)} %get-tuple-element.22.early_gate, ...), custom_call_target="tpu_custom_call" | custom-call | flops 1000000000 | bytes 5000000 | tf_op jit(solution)/shard_map/own_states/pallas_call | solution.py:154
  7.1 0.0 collective-permute-done.other_ref
  7.1 1.0 %combine.1 = (f32[16,72,128]{2,1,0:T(8,128)}, f32[16,72,128]{2,1,0:T(8,128)}) custom-call(s32[1]{0:T(128)} %bitcast.core_ref, f32[16,72,128]{2,1,0:T(8,128)S(1)} %own_states.1.mine_ref, f32[16,72,128]{2,1,0:T(8,128)S(1)} %collective-permute-done.other_ref), custom_call_target="tpu_custom_call" | custom-call | tf_op jit(solution)/shard_map/combine/pallas_call | solution.py:186
  8.1 7.9 %all-to-all-start = ((f32[16,72,128]{2,1,0:T(8,128)}), f32[16,72,128]{2,1,0:T(8,128)S(1)}, u32[]{:S(2)}, u32[]{:S(2)}) async-start(f32[16,72,128]{2,1,0:T(8,128)} %get-tuple-element.29), calls=%async_computation | async-start | bytes 1179648 | tf_op jit(solution)/shard_map/all_to_all | solution.py:383
  16.0 0.4 collective-permute-start.1
  16.4 8.1 %own_local.1 = (bf16[512,1024]{1,0:T(8,128)(2,1)S(1)}, bf16[512,1024]{1,0:T(8,128)(2,1)S(1)}, f32[8,128]{1,0:T(8,128)S(1)}) custom-call(s32[1]{0:T(128)} %bitcast.core_ref, bf16[512,2048]{1,0:T(8,128)(2,1)} %query_hbm.3, bf16[512,2048]{1,0:T(8,128)(2,1)} %key_hbm.7, bf16[512,2048]{1,0:T(8,128)(2,1)} %value_hbm.7, f32[512,2048]{1,0:T(8,128)} %gate_hbm.7, ...), custom_call_target="tpu_custom_call" | custom-call | flops 4000000000 | bytes 8000000 | tf_op jit(solution)/shard_map/own_local/pallas_call | solution.py:296
  24.5 3.3 %all-to-all-done.in_ref = f32[16,72,128]{2,1,0:T(8,128)S(1)} async-done(((f32[16,72,128]{2,1,0:T(8,128)}), f32[16,72,128]{2,1,0:T(8,128)S(1)}, u32[]{:S(2)}, u32[]{:S(2)}) %all-to-all-start) | async-done | bytes 589856 | tf_op jit(solution)/shard_map/all_to_all | solution.py:383
  27.8 0.8 %prefix.1 = f32[16,64,128]{2,1,0:T(8,128)} custom-call(f32[16,72,128]{2,1,0:T(8,128)S(1)} %all-to-all-done.in_ref, f32[8,128]{1,0:T(8,128)S(1)} %get-tuple-element.30._), custom_call_target="tpu_custom_call" | custom-call | tf_op jit(solution)/shard_map/prefix/pallas_call | solution.py:215
  28.6 3.6 %all-to-all-start.1 = ((f32[16,64,128]{2,1,0:T(8,128)}), f32[16,64,128]{2,1,0:T(8,128)S(1)}, u32[]{:S(2)}, u32[]{:S(2)}) async-start(f32[16,64,128]{2,1,0:T(8,128)} %prefix.1), calls=%async_computation.1 | async-start | bytes 1048576 | tf_op jit(solution)/shard_map/all_to_all | solution.py:383
  32.2 0.0 collective-permute-done.1.init_any
  32.2 9.0 %rest_local.1 = (bf16[512,1024]{1,0:T(8,128)(2,1)}, bf16[512,1024]{1,0:T(8,128)(2,1)}, f32[8,128]{1,0:T(8,128)S(1)}) custom-call(s32[1]{0:T(128)} %bitcast.core_ref, bf16[512,2048]{1,0:T(8,128)(2,1)} %query_hbm.3, bf16[512,2048]{1,0:T(8,128)(2,1)} %key_hbm.7, bf16[512,2048]{1,0:T(8,128)(2,1)} %value_hbm.7, f32[512,2048]{1,0:T(8,128)} %gate_hbm.7, ...), custom_call_target="tpu_custom_call" | custom-call | flops 4000000000 | bytes 8000000 | tf_op jit(solution)/shard_map/rest_local/pallas_call | solution.py:296
  41.2 1.2 %all-to-all-done.1 = f32[16,64,128]{2,1,0:T(8,128)S(1)} async-done(((f32[16,64,128]{2,1,0:T(8,128)}), f32[16,64,128]{2,1,0:T(8,128)S(1)}, u32[]{:S(2)}, u32[]{:S(2)}) %all-to-all-start.1) | async-done | bytes 524320 | tf_op jit(solution)/shard_map/all_to_all | solution.py:383
  42.4 2.3 %collective-permute-start.2 = (f32[1024,128]{1,0:T(8,128)S(1)}, f32[1024,128]{1,0:T(8,128)S(1)}, u32[]{:S(2)}, u32[]{:S(2)}) collective-permute-start(f32[1024,128]{1,0:T(8,128)S(1)} %bitcast.2), channel_id=1, source_target_pairs={{0,4},{4,0},{8,12},{12,8},{16,20},{20,16},{24,28},{28,24},{32,36},... | collective-permute-start | bytes 1572872 | tf_op jit(solution)/shard_map/ppermute | solution.py:396
  44.7 2.0 %own_final.1 = (bf16[512,2048]{1,0:T(8,128)(2,1)}, bf16[512,1024]{1,0:T(8,128)(2,1)S(1)}, bf16[512,1024]{1,0:T(8,128)(2,1)S(1)}) custom-call(s32[1]{0:T(128)} %bitcast.core_ref, bf16[512,1024]{1,0:T(8,128)(2,1)S(1)} %get-tuple-element.27.local, bf16[512,1024]{1,0:T(8,128)(2,1)S(1)} %get-tuple-element.28.decayed, f32[1024,128]{1,0:T(8,128)S(1)} %bitcast.3, ...), custom_call_target="tpu_custom_call" | custom-call | flops 1000000000 | bytes 4000000 | tf_op jit(solution)/shard_map/own_final/pallas_call | solution.py:339
  46.7 0.0 collective-permute-done.2.entry
  46.7 1.2 %rest_final.1 = bf16[512,2048]{1,0:T(8,128)(2,1)} custom-call(s32[1]{0:T(128)} %bitcast.core_ref, bf16[512,1024]{1,0:T(8,128)(2,1)S(1)} %get-tuple-element.36.local, bf16[512,1024]{1,0:T(8,128)(2,1)S(1)} %get-tuple-element.37.decayed, f32[1024,128]{1,0:T(8,128)S(1)} %collective-permute-done.2.entry, ...), custom_call_target="tpu_custom_call", output_to_operand_aliasing={{}: (4, {})} | custom-call | flops 1000000000 | bytes 4000000 | tf_op jit(solution)/shard_map/rest_final/pallas_call | solution.py:362
Async XLA Ops:
  3.4 3.7 %collective-permute-start = (f32[16,72,128]{2,1,0:T(8,128)S(1)}, f32[16,72,128]{2,1,0:T(8,128)S(1)}, u32[]{:S(2)}, u32[]{:S(2)}) collective-permute-start(f32[16,72,128]{2,1,0:T(8,128)S(1)} %get-tuple-element.25), channel_id=1, source_target_pairs={{0,4},{4,0},{8,12},{12,8},{16,20},{20,16},{24,28},{28,24},{32,36},... | collective-permute-start | bytes 1769480 | tf_op jit(solution)/shard_map/ppermute | solution.py:386
  8.1 19.6 %all-to-all-start = ((f32[16,72,128]{2,1,0:T(8,128)}), f32[16,72,128]{2,1,0:T(8,128)S(1)}, u32[]{:S(2)}, u32[]{:S(2)}) async-start(f32[16,72,128]{2,1,0:T(8,128)} %get-tuple-element.29), calls=%async_computation | async-start | bytes 1179648 | tf_op jit(solution)/shard_map/all_to_all | solution.py:383
  16.0 16.2 %collective-permute-start.1 = (f32[16,72,128]{2,1,0:T(8,128)S(1)}, f32[16,72,128]{2,1,0:T(8,128)}, u32[]{:S(2)}, u32[]{:S(2)}) collective-permute-start(f32[16,72,128]{2,1,0:T(8,128)S(1)} %own_states.1.mine_ref), channel_id=1, source_target_pairs={{0,4},{4,0},{8,12},{12,8},{16,20},{20,16},{24,28},{28,24},{32,36},... | collective-permute-start | bytes 1769480 | tf_op jit(solution)/shard_map/ppermute | solution.py:388
  28.6 13.8 %all-to-all-start.1 = ((f32[16,64,128]{2,1,0:T(8,128)}), f32[16,64,128]{2,1,0:T(8,128)S(1)}, u32[]{:S(2)}, u32[]{:S(2)}) async-start(f32[16,64,128]{2,1,0:T(8,128)} %prefix.1), calls=%async_computation.1 | async-start | bytes 1048576 | tf_op jit(solution)/shard_map/all_to_all | solution.py:383
  42.4 4.3 %collective-permute-start.2 = (f32[1024,128]{1,0:T(8,128)S(1)}, f32[1024,128]{1,0:T(8,128)S(1)}, u32[]{:S(2)}, u32[]{:S(2)}) collective-permute-start(f32[1024,128]{1,0:T(8,128)S(1)} %bitcast.2), channel_id=1, source_target_pairs={{0,4},{4,0},{8,12},{12,8},{16,20},{20,16},{24,28},{28,24},{32,36},... | collective-permute-start | bytes 1572872 | tf_op jit(solution)/shard_map/ppermute | solution.py:396

commit v2 on v1

--- a/solution.py
+++ b/solution.py
@@ -18,6 +18,8 @@
 LANES = HEADS_STEP * DK
 STEPS = HALF // HEADS_STEP
 EARLY = 2
+WIDE = 512
+LOCAL_STEPS = WIDTH // WIDE
 CHUNKS = 4
 ROWS = 64
 SLICE = ROWS + 8
@@ -59,8 +61,8 @@
     return dot(ones, jnp.concatenate([high, low], axis=0))
 
 
-def columns(half, step):
-    return pl.ds(pl.multiple_of(half * WIDTH + step * LANES, LANES), LANES)
+def columns(half, step, lanes=LANES):
+    return pl.ds(pl.multiple_of(half * WIDTH + step * lanes, lanes), lanes)
 
 
 def states_step(step, gate_ref, key_ref, value_ref, out_ref):
@@ -87,17 +89,20 @@
             out_ref[at, ROWS:SLICE, :] = jnp.broadcast_to(total[head], (SLICE - ROWS, DK))
 
 
-def column_copies(half, steps, sources, targets, sems):
+def column_copies(half, steps, sources, targets, sems, lanes=LANES):
     copies = []
     for step in steps:
         for source, target in zip(sources, targets):
-            at = pl.ds(step * LANES, LANES)
+            at = pl.ds(step * lanes, lanes)
             copies.append(
-                pltpu.make_async_copy(source.at[:, columns(half, step)], target.at[:, at], sems.at[len(copies)])
+                pltpu.make_async_copy(source.at[:, columns(half, step, lanes)], target.at[:, at], sems.at[len(copies)])
             )
+    return [copies[i : i + len(sources)] for i in range(0, len(copies), len(sources))]
+
+
+def start_all(copies):
     for copy in copies:
         copy.start()
-    return [copies[i : i + len(sources)] for i in range(0, len(copies), len(sources))]
 
 
 def wait_all(copies):
@@ -111,6 +116,8 @@
     sources = (gate_hbm, key_hbm, value_hbm)
     mine = column_copies(1 - core_ref[0], range(STEPS), sources, (gate, key, value), sems)
     early = column_copies(core_ref[0], range(EARLY), sources, (own_gate, own_key, own_value), own_sems)
+    for copies in mine + early:
+        start_all(copies)
     for step in range(STEPS):
         wait_all(mine[step])
         states_step(step, gate, key, value, out_ref)
@@ -141,6 +148,8 @@
     mine = column_copies(
         core_ref[0], range(EARLY, STEPS), (gate_hbm, key_hbm, value_hbm), (gate, key, value), sems
     )
+    for copies in mine:
+        start_all(copies)
     for step in range(EARLY):
         states_step(step, early_gate, early_key, early_value, out_ref)
     for step in range(EARLY, STEPS):
@@ -164,37 +173,52 @@
     )(core, in_hbm(gate), in_hbm(keys), in_hbm(values), *map(in_vmem, early))
 
 
-def combine_kernel(core_ref, mine_ref, other_ref, out_hbm, other_hbm, out_ref, sems):
-    copies = [pltpu.make_async_copy(other_ref, other_hbm, sems.at[CHUNKS])]
-    copies[0].start()
+def combine_kernel(core_ref, mine_ref, other_ref, out_ref, keep_ref):
     first = core_ref[0] == 0
-    length = mine_ref.shape[0] // CHUNKS
-    for chunk in range(CHUNKS):
-        at = pl.ds(chunk * length, length)
-        mine_total = mine_ref[at, ROWS:SLICE, :]
-        other_total = other_ref[at, ROWS:SLICE, :]
-        mine_weight = jnp.where(first, jnp.exp2(other_total), 1.0)[:, 0:1]
-        other_weight = jnp.where(first, 1.0, jnp.exp2(mine_total))[:, 0:1]
-        out_ref[at, 0:ROWS, :] = mine_ref[at, 0:ROWS, :] * mine_weight + other_ref[at, 0:ROWS, :] * other_weight
-        out_ref[at, ROWS:SLICE, :] = mine_total + other_total
-        copies.append(pltpu.make_async_copy(out_ref.at[at], out_hbm.at[at], sems.at[chunk]))
-        copies[-1].start()
-    wait_all(copies)
+    mine_total = mine_ref[:, ROWS:SLICE, :]
+    other_total = other_ref[:, ROWS:SLICE, :]
+    mine_weight = jnp.where(first, jnp.exp2(other_total), 1.0)[:, 0:1]
+    other_weight = jnp.where(first, 1.0, jnp.exp2(mine_total))[:, 0:1]
+    mine = mine_ref[:, 0:ROWS, :]
+    other = other_ref[:, 0:ROWS, :]
+    out_ref[:, 0:ROWS, :] = mine * mine_weight + other * other_weight
+    out_ref[:, ROWS:SLICE, :] = mine_total + other_total
+    keep_ref[:, 0:ROWS, :] = jnp.where(first, mine, other)
+    keep_ref[:, ROWS:SLICE, :] = jnp.where(first, mine_total, other_total)
 
 
 def combine(core, mine, other):
     return pl.pallas_call(
         combine_kernel,
         in_specs=[SMEM, VMEM, VMEM],
-        out_specs=[HBM, HBM],
-        out_shape=[pltpu.HBM(mine.shape, jnp.float32)] * 2,
-        scratch_shapes=[pltpu.VMEM(mine.shape, jnp.float32), pltpu.SemaphoreType.DMA((CHUNKS + 1,))],
+        out_specs=[VMEM, VMEM],
+        out_shape=[pltpu.VMEM(mine.shape, jnp.float32)] * 2,
         compiler_params=pltpu.CompilerParams(vmem_limit_bytes=4 << 20),
         name="combine",
     )(core, in_vmem(mine), in_vmem(other))
 
 
-def prefix_kernel(in_ref, _, out_hbm, out_ref, sems):
+def advance_kernel(core_ref, entry_ref, keep_ref, mine_ref, sent_ref):
+    first = core_ref[0] == 0
+    entry = entry_ref[...]
+    advanced = entry * jnp.exp2(keep_ref[:, ROWS : ROWS + 1, :]) + keep_ref[:, 0:ROWS, :]
+    mine_ref[...] = jnp.where(first, entry, advanced)
+    sent_ref[...] = jnp.where(first, advanced, entry)
+
+
+def advance(core, entry, keep):
+    return pl.pallas_call(
+        advance_kernel,
+        in_specs=[SMEM, VMEM, VMEM],
+        out_specs=[VMEM, VMEM],
+        out_shape=[pltpu.VMEM(entry.shape, jnp.float32)] * 2,
+        compiler_params=pltpu.CompilerParams(vmem_limit_bytes=4 << 20),
+        name="advance",
+    )(core, in_vmem(entry), in_vmem(keep))
+
+
+def prefix_kernel(in_ref, out_hbm, done_ref, out_ref, sems):
+    done_ref[...] = jnp.zeros_like(done_ref)
     running = jnp.zeros((ROWS, DK), jnp.float32)
     chips = in_ref.shape[0]
     copies = []
@@ -210,99 +234,128 @@
     wait_all(copies)
 
 
-def prefix(received, after):
+def prefix(received):
     shape = (received.shape[0], ROWS, DK)
     return pl.pallas_call(
         prefix_kernel,
-        in_specs=[VMEM, ANY],
-        out_specs=HBM,
-        out_shape=pltpu.HBM(shape, jnp.float32),
+        in_specs=[VMEM],
+        out_specs=[HBM, VMEM],
+        out_shape=[pltpu.HBM(shape, jnp.float32), jax.ShapeDtypeStruct((8, DK), jnp.float32)],
         scratch_shapes=[pltpu.VMEM(shape, jnp.float32), pltpu.SemaphoreType.DMA((shape[0] // CHUNKS,))],
         compiler_params=pltpu.CompilerParams(vmem_limit_bytes=4 << 20),
         name="prefix",
-    )(in_vmem(received), after)
-
-
-def local_step(step, second, query_ref, key_ref, value_ref, gate_ref, init_ref, local_ref, decayed_ref):
+    )(in_vmem(received))
+
+
+def local_step(step, waits, query_ref, key_ref, value_ref, gate_ref, local_ref, decayed_ref, stored):
     ones = triangle(False)
     row = lax.broadcasted_iota(jnp.int32, (GROUP, GROUP), 0)
     col = lax.broadcasted_iota(jnp.int32, (GROUP, GROUP), 1)
     causal = row >= col
-    cols = pl.ds(step * LANES, LANES)
-    state, total = [], []
-    for head in range(HEADS_STEP):
-        at = 2 * (step * HEADS_STEP + head)
-        start = jnp.concatenate([init_ref[at, 0:ROWS, :], init_ref[at + 1, 0:ROWS, :]], axis=0)
-        state.append(jnp.where(second, start, 0.0))
-        total.append(jnp.where(second, init_ref[at, ROWS : ROWS + 1, :], 0.0))
-    groups = gate_ref.shape[0] // GROUP
-    for group in range(groups):
-        rows = pl.ds(group * GROUP, GROUP)
-        inclusive = partial_sums(ones, gate_ref[rows, cols] * LOG2E)
-        gamma = inclusive[GROUP - 1 : GROUP]
-        decay = jnp.exp2(gamma)
-        query = query_ref[rows, cols].astype(jnp.float32) * jnp.exp2(inclusive + LOG2_SCALE)
-        key = key_ref[rows, cols].astype(jnp.float32) * jnp.exp2(-inclusive)
-        query_scaled = query.astype(jnp.bfloat16)
-        key_inverse = key.astype(jnp.bfloat16)
-        to_end = (key * decay).astype(jnp.bfloat16)
-        before = jnp.exp2(jnp.concatenate(total, axis=1))
-        decayed_ref[rows, cols] = (query * before).astype(jnp.bfloat16)
-        for head in range(HEADS_STEP):
-            at = slice(head * DK, (head + 1) * DK)
-            head_cols = pl.ds(step * LANES + head * DV, DV)
-            value = value_ref[rows, head_cols]
-            scores = dot(query_scaled[:, at], key_inverse[:, at], NT)
-            scores = jnp.where(causal, scores, 0.0).astype(jnp.bfloat16)
-            out = dot(scores, value) + dot(query_scaled[:, at], state[head].astype(jnp.bfloat16), NT)
-            local_ref[rows, head_cols] = out.astype(local_ref.dtype)
-            if group < groups - 1:
-                state[head] = state[head] * decay[:, at] + dot(value, to_end[:, at], TN)
-                total[head] = total[head] + gamma[:, at]
-
-
-def local_kernel(rest, core_ref, query_hbm, key_hbm, value_hbm, gate_hbm, init_any, local_out, decayed_out, done_ref, *refs):
-    query, key, value, gate, init, sems, init_sem = refs[:7]
+    cols = pl.ds(step * WIDE, WIDE)
+    groups = range(gate_ref.shape[0] // GROUP)
+    heads = range(WIDE // DK)
+    rows = [pl.ds(group * GROUP, GROUP) for group in groups]
+    at = [slice(head * DK, (head + 1) * DK) for head in heads]
+    waits[0]()
+    sums = [partial_sums(ones, gate_ref[rows[group], cols] * LOG2E) for group in groups]
+    gamma = [inclusive[GROUP - 1 : GROUP] for inclusive in sums]
+    decay = [jnp.exp2(total) for total in gamma]
+    waits[1]()
+    queries, keys, to_end = [], [], []
+    before = None
+    for group in groups:
+        query = query_ref[rows[group], cols].astype(jnp.float32) * jnp.exp2(sums[group] + LOG2_SCALE)
+        key = key_ref[rows[group], cols].astype(jnp.float32) * jnp.exp2(-sums[group])
+        queries.append(query.astype(jnp.bfloat16))
+        keys.append(key.astype(jnp.bfloat16))
+        to_end.append((key * decay[group]).astype(jnp.bfloat16))
+        if group == 0:
+            decayed_ref[rows[group], cols] = queries[group]
+            before = gamma[group]
+        else:
+            decayed_ref[rows[group], cols] = (query * jnp.exp2(before)).astype(jnp.bfloat16)
+            before = before + gamma[group]
+    stored(0, cols)
+    value_cols = [pl.ds(step * WIDE + head * DV, DV) for head in heads]
+    scores = [[dot(queries[group][:, at[head]], keys[group][:, at[head]], NT) for head in heads] for group in groups]
+    scores = [[jnp.where(causal, x, 0.0).astype(jnp.bfloat16) for x in line] for line in scores]
+    updates = [
+        [dot(value_ref[rows[group], value_cols[head]], to_end[group][:, at[head]], TN) for head in heads]
+        for group in groups[:-1]
+    ]
+    for head in heads:
+        state = None
+        for group in groups:
+            value = value_ref[rows[group], value_cols[head]]
+            if group == 0:
+                out = dot(scores[group][head], value)
+                state = updates[group][head]
+            else:
+                left = jnp.concatenate([scores[group][head], queries[group][:, at[head]]], axis=1)
+                out = dot(left, jnp.concatenate([value, state.astype(jnp.bfloat16).T], axis=0))
+                if group < groups[-1]:
+                    state = state * decay[group][:, at[head]] + updates[group][head]
+            local_ref[rows[group], value_cols[head]] = out.astype(local_ref.dtype)
+    stored(1, cols)
+
+
+def local_kernel(*refs):
+    core_ref, query_hbm, key_hbm, value_hbm, gate_hbm, _ = refs[:6]
+    own_local, own_decayed, rest_local_hbm, rest_decayed_hbm, done_ref = refs[6:11]
+    query, key, value, gate, rest_local, rest_decayed, first, sems, first_sem, store_sems = refs[11:]
     core = core_ref[0]
-    half = 1 - core if rest else core
-    fetch = pltpu.make_async_copy(init_any, init, init_sem)
-    fetch.start()
-    copies = column_copies(
-        half, range(STEPS), (gate_hbm, query_hbm, key_hbm, value_hbm), (gate, query, key, value), sems
-    )
-    fetch.wait()
-    local_ref, decayed_ref = refs[7:9] if rest else (local_out, decayed_out)
+    steps = range(LOCAL_STEPS)
+    queue = []
+    for i, half in ((0, core), (1, 1 - core)):
+        targets = tuple(x.at[i] for x in (gate, key, query, value))
+        queue += column_copies(half, steps, (gate_hbm, key_hbm, query_hbm, value_hbm), targets, sems.at[i], WIDE)
+    early = pltpu.make_async_copy(gate_hbm.at[0:8, 0:DK], first, first_sem)
+    early.start()
+    start_all(queue[0])
+    early.wait()
+    start_all(queue[1])
     stores = []
-    for step in range(STEPS):
-        wait_all(copies[step])
-        local_step(step, core == 1, query, key, value, gate, init, local_ref, decayed_ref)
-        if rest:
-            at = pl.ds(step * LANES, LANES)
-            for ref, out in ((local_ref, local_out), (decayed_ref, decayed_out)):
-                stores.append(pltpu.make_async_copy(ref.at[:, at], out.at[:, at], refs[9].at[len(stores)]))
-                stores[-1].start()
+
+    def store(which, cols):
+        ref, out = ((rest_decayed, rest_decayed_hbm), (rest_local, rest_local_hbm))[which]
+        stores.append(pltpu.make_async_copy(ref.at[:, cols], out.at[:, cols], store_sems.at[len(stores)]))
+        stores[-1].start()
+
+    for i, out, decayed, stored in (
+        (0, own_local, own_decayed, lambda which, cols: None),
+        (1, rest_local, rest_decayed, store),
+    ):
+        inputs = [x.at[i] for x in (query, key, value, gate)]
+        for step in steps:
+            place = i * LOCAL_STEPS + step
+
+            def gates(place=place):
+                queue[place][0].wait()
+                if place + 2 < len(queue):
+                    start_all(queue[place + 2])
+
+            local_step(step, (gates, lambda place=place: wait_all(queue[place][1:])), *inputs, out, decayed, stored)
+    done_ref[...] = jnp.zeros_like(done_ref)
     wait_all(stores)
-    done_ref[...] = jnp.zeros_like(done_ref)
-
-
-def local_part(rest, core, queries, keys, values, gate, init):
+
+
+def local_part(core, queries, keys, values, gate, after):
     tokens = keys.shape[0]
-    place = pltpu.HBM if rest else pltpu.VMEM
     half = ((tokens, WIDTH), jnp.bfloat16)
-    scratch = [pltpu.VMEM((tokens, WIDTH), x.dtype) for x in (queries, keys, values, gate)]
-    scratch += [pltpu.VMEM(init.shape, init.dtype), pltpu.SemaphoreType.DMA((4 * STEPS,)), pltpu.SemaphoreType.DMA]
-    if rest:
-        scratch += [pltpu.VMEM(*half)] * 2 + [pltpu.SemaphoreType.DMA((2 * STEPS,))]
-    return pl.pallas_call(
-        functools.partial(local_kernel, rest),
-        in_specs=[SMEM] + [HBM] * 5,
-        out_specs=[HBM if rest else VMEM] * 2 + [VMEM],
-        out_shape=[place(*half)] * 2 + [jax.ShapeDtypeStruct((8, DK), jnp.float32)],
-        scratch_shapes=scratch,
-        compiler_params=pltpu.CompilerParams(vmem_limit_bytes=12 << 20),
-        cost_estimate=pl.CostEstimate(flops=4 * 10**9, bytes_accessed=8 * 10**6, transcendentals=10**6),
-        name="rest_local" if rest else "own_local",
-    )(core, in_hbm(queries), in_hbm(keys), in_hbm(values), in_hbm(gate), in_hbm(init))
+    return pl.pallas_call(
+        local_kernel,
+        in_specs=[SMEM] + [HBM] * 4 + [ANY],
+        out_specs=[VMEM, VMEM, HBM, HBM, VMEM],
+        out_shape=[pltpu.VMEM(*half)] * 2 + [pltpu.HBM(*half)] * 2 + [jax.ShapeDtypeStruct((8, DK), jnp.float32)],
+        scratch_shapes=[pltpu.VMEM((2, tokens, WIDTH), x.dtype) for x in (queries, keys, values, gate)]
+        + [pltpu.VMEM(*half)] * 2
+        + [pltpu.VMEM((8, DK), jnp.float32), pltpu.SemaphoreType.DMA((2, 4 * LOCAL_STEPS))]
+        + [pltpu.SemaphoreType.DMA, pltpu.SemaphoreType.DMA((2 * LOCAL_STEPS,))],
+        compiler_params=pltpu.CompilerParams(vmem_limit_bytes=32 << 20),
+        cost_estimate=pl.CostEstimate(flops=8 * 10**9, bytes_accessed=16 * 10**6, transcendentals=10**6),
+        name="local_part",
+    )(core, in_hbm(queries), in_hbm(keys), in_hbm(values), in_hbm(gate), after)
 
 
 def final_step(step, local_ref, decayed_ref, entry_ref, out_ref):
@@ -385,16 +438,15 @@
     rest, *early = rest_states(core, log_gate, keys, values)
     own_other = lax.ppermute(rest, "seq", swap)
     own = own_states(core, log_gate, keys, values, early)
-    rest_other = lax.ppermute(own, "seq", swap)
-    combined, own_other = combine(core, own, own_other)
-    received = exchange(combined)
-    own_local, own_decayed, own_done = local_part(False, core, queries, keys, values, log_gate, own_other)
-    own_entry = exchange(prefix(received, own_done))
-    rest_local, rest_decayed, rest_done = local_part(True, core, queries, keys, values, log_gate, rest_other)
-    own_entry, rest_done = lax.optimization_barrier((own_entry, rest_done))
+    combined, keep = combine(core, own, own_other)
+    entries, after = prefix(exchange(combined))
+    entry = exchange(entries)
+    own_local, own_decayed, rest_local, rest_decayed, after = local_part(core, queries, keys, values, log_gate, after)
+    entry, after = lax.optimization_barrier((entry, after))
+    own_entry, sent = advance(core, entry, keep)
+    rest_entry = lax.ppermute(sent, "seq", swap).reshape(HALF * DV, DK)
     own_entry = own_entry.reshape(HALF * DV, DK)
-    rest_entry = lax.ppermute(own_entry, "seq", swap)
-    out, local, decayed = own_final(core, own_local, own_decayed, own_entry, rest_local, rest_decayed, rest_done)
+    out, local, decayed = own_final(core, own_local, own_decayed, own_entry, rest_local, rest_decayed, after)
     return rest_final(core, local, decayed, rest_entry, out)
 
 

time: 48.3 us -> 47.7 us (0.988)
  blocking collectives: 0 us -> 19.7 us
  Pallas kernels: 27.7 us -> 17.8 us
  starting transfers between devices: 15.6 us -> 7.19 us
  waiting for transfers between devices: 4.51 us -> 2.51 us
    all_to_all x0 -> x1, blocking collectives: none -> 19.7 us  [exchange(): lax.all_to_all(blocks, 'seq', split_axis=0, concat_axis=0, axis_index_gro...]
    pallas_call x4, Pallas kernels: 18.9 us -> 9.02 us  [the longest x1 7.91 us: local_part(): pl.pallas_call(local_kernel, in_specs=[SMEM] + [HBM] * 4 + [ANY], out_spe...]
    all_to_all x2 -> x1, starting transfers between devices: 11.4 us -> 3.59 us  [exchange(): lax.all_to_all(blocks, 'seq', split_axis=0, concat_axis=0, axis_index_gro...]
    all_to_all x2 -> x1, waiting for transfers between devices: 4.5 us -> 2.51 us  [exchange(): lax.all_to_all(blocks, 'seq', split_axis=0, concat_axis=0, axis_index_gro...]
    ppermute x2 -> x1, starting transfers between devices: 2.66 us -> 2.1 us  [on_device(): rest_entry = lax.ppermute(sent, 'seq', swap).reshape(HALF * DV, DK)]
  transfers between devices with their start and end apart: 5 -> 3, of which waited for: 2 -> 1; matrix products, arithmetic and copies ran while one was open for 0% -> 0% of each run, Pallas kernels for 46% -> 26%
where the time goes in v2:
time: 47.7 us; the launch traced here: 47.3 us
  blocking collectives  19.7 us (41%)
  Pallas kernels  17.8 us (37%)
  starting transfers between devices  7.19 us (15%)
  waiting for transfers between devices  2.51 us (5%)
    all_to_all x1, blocking collectives, exchange(): lax.all_to_all(blocks, 'seq', split_axis=0, concat_axis=0, axis_index_gro...  19.7 us
    pallas_call x1, Pallas kernels, local_part(): pl.pallas_call(local_kernel, in_specs=[SMEM] + [HBM] * 4 + [ANY], out_spe...  7.91 us
    all_to_all x1, starting transfers between devices, exchange(): lax.all_to_all(blocks, 'seq', split_axis=0, concat_axis=0, axis_index_gro...  3.59 us
    pallas_call x1, Pallas kernels, rest_states(): pl.pallas_call(rest_states_kernel, in_specs=[SMEM, HBM, HBM, HBM], out_sp...  3.35 us
    all_to_all x1, waiting for transfers between devices, exchange(): lax.all_to_all(blocks, 'seq', split_axis=0, concat_axis=0, axis_index_gro...  2.51 us
    pallas_call x1, Pallas kernels, own_states(): pl.pallas_call(own_states_kernel, in_specs=[SMEM, HBM, HBM, HBM] + [VMEM]...  2.2 us
    ppermute x1, starting transfers between devices, on_device(): rest_entry = lax.ppermute(sent, 'seq', swap).reshape(HALF * DV, DK)  2.1 us
    pallas_call x1, Pallas kernels, own_final(): pl.pallas_call(own_final_kernel, in_specs=[SMEM] + [VMEM] * 3 + [HBM] * 2...  2.01 us
  transfers between devices with their start and end apart: 3, of which 1 were waited for; matrix products, arithmetic and copies ran while one was open for 0% of the time, Pallas kernels for 26%

profile of v2, /device:TPU:1, one launch (start us, length us, event | category | flops | bytes accessed | tf_op | source)
XLA Modules:
  0.0 47.3 jit_solution(7914461304548549682)
XLA Ops:
  0.0 3.4 %rest_states.1 = (f32[16,72,128]{2,1,0:T(8,128)S(1)}, f32[512,512]{1,0:T(8,128)S(1)}, bf16[512,512]{1,0:T(8,128)(2,1)S(1)}, bf16[512,512]{1,0:T(8,128)(2,1)S(1)}) custom-call(s32[1]{0:T(128)} %bitcast.core_ref.refs_0_, f32[512,2048]{1,0:T(8,128)} %refs_4_.1, bf16[512,2048]{1,0:T(8,128)(2,1)} %refs_2_.1, bf16[512,2048]{1,0:T(8,128)(2,1)} %refs_3_.1), custom_call_target="tpu_custom_call" | custom-call | flops 1000000000 | bytes 9000000 | tf_op jit(solution)/shard_map/rest_states/pallas_call | solution.py:131
  3.4 1.5 %collective-permute-start = (f32[16,72,128]{2,1,0:T(8,128)S(1)}, f32[16,72,128]{2,1,0:T(8,128)S(1)}, u32[]{:S(2)}, u32[]{:S(2)}) collective-permute-start(f32[16,72,128]{2,1,0:T(8,128)S(1)} %get-tuple-element.28), channel_id=1, source_target_pairs={{0,4},{4,0},{8,12},{12,8},{16,20},{20,16},{24,28},{28,24},{32,36},... | collective-permute-start | bytes 1769480 | tf_op jit(solution)/shard_map/ppermute | solution.py:439
  4.9 2.2 %own_states.1.mine_ref = f32[16,72,128]{2,1,0:T(8,128)S(1)} custom-call(s32[1]{0:T(128)} %bitcast.core_ref.refs_0_, f32[512,2048]{1,0:T(8,128)} %refs_4_.1, bf16[512,2048]{1,0:T(8,128)(2,1)} %refs_2_.1, bf16[512,2048]{1,0:T(8,128)(2,1)} %refs_3_.1, f32[512,512]{1,0:T(8,128)S(1)} %get-tuple-element.25.early_gate, ...), custom_call_target="tpu_custom_call" | custom-call | flops 1000000000 | bytes 5000000 | tf_op jit(solution)/shard_map/own_states/pallas_call | solution.py:163
  7.1 0.0 collective-permute-done.other_ref
  7.1 0.1 combine.1
  7.2 19.7 %all_to_all.10.in_ref = f32[16,72,128]{2,1,0:T(8,128)S(1)} all-to-all(f32[16,72,128]{2,1,0:T(8,128)S(1)} %get-tuple-element.29), channel_id=1, replica_groups={{0,8,16,24,32,40,48,56,64,72,80,88,96,104,112,120},{4,12,20,28,36,44,52..., dimensions={0} | all-to-all | bytes 1179648 | tf_op jit(solution)/shard_map/all_to_all | solution.py:436
  27.0 0.8 %prefix.1 = (f32[16,64,128]{2,1,0:T(8,128)}, f32[8,128]{1,0:T(8,128)S(1)}) custom-call(f32[16,72,128]{2,1,0:T(8,128)S(1)} %all_to_all.10.in_ref), custom_call_target="tpu_custom_call" | custom-call | tf_op jit(solution)/shard_map/prefix/pallas_call | solution.py:239
  27.8 3.6 %all-to-all-start.1 = ((f32[16,64,128]{2,1,0:T(8,128)}), f32[16,64,128]{2,1,0:T(8,128)S(1)}, u32[]{:S(2)}, u32[]{:S(2)}) async-start(f32[16,64,128]{2,1,0:T(8,128)} %get-tuple-element.33), calls=%async_computation.1 | async-start | bytes 1048576 | tf_op jit(solution)/shard_map/all_to_all | solution.py:436
  31.4 7.9 %local_part.1 = (bf16[512,1024]{1,0:T(8,128)(2,1)S(1)}, bf16[512,1024]{1,0:T(8,128)(2,1)S(1)}, bf16[512,1024]{1,0:T(8,128)(2,1)}, bf16[512,1024]{1,0:T(8,128)(2,1)}, f32[8,128]{1,0:T(8,128)S(1)}) custom-call(s32[1]{0:T(128)} %bitcast.core_ref.refs_0_, bf16[512,2048]{1,0:T(8,128)(2,1)} %refs_1_.1, bf16[512,2048]{1,0:T(8,128)(2,1)} %refs_2_.1, ...), custom_call_target="tpu_custom_call" | custom-call | flops 8000000000 | bytes 16000000 | tf_op jit(solution)/shard_map/local_part/pallas_call | solution.py:346
  39.3 2.5 %all-to-all-done.1.entry_ref = f32[16,64,128]{2,1,0:T(8,128)S(1)} async-done(((f32[16,64,128]{2,1,0:T(8,128)}), f32[16,64,128]{2,1,0:T(8,128)S(1)}, u32[]{:S(2)}, u32[]{:S(2)}) %all-to-all-start.1) | async-done | bytes 524320 | tf_op jit(solution)/shard_map/all_to_all | solution.py:436
  41.8 0.1 advance.1
  42.0 2.1 %collective-permute-start.1 = (f32[16,64,128]{2,1,0:T(8,128)S(1)}, f32[16,64,128]{2,1,0:T(8,128)S(1)}, u32[]{:S(2)}, u32[]{:S(2)}) collective-permute-start(f32[16,64,128]{2,1,0:T(8,128)S(1)} %get-tuple-element.43), channel_id=1, source_target_pairs={{0,4},{4,0},{8,12},{12,8},{16,20},{20,16},{24,28},{28,24},{32,36},... | collective-permute-start | bytes 1572872 | tf_op jit(solution)/shard_map/ppermute | solution.py:447
  44.1 2.0 %own_final.1 = (bf16[512,2048]{1,0:T(8,128)(2,1)}, bf16[512,1024]{1,0:T(8,128)(2,1)S(1)}, bf16[512,1024]{1,0:T(8,128)(2,1)S(1)}) custom-call(s32[1]{0:T(128)} %bitcast.core_ref.refs_0_, bf16[512,1024]{1,0:T(8,128)(2,1)S(1)} %get-tuple-element.31.local, bf16[512,1024]{1,0:T(8,128)(2,1)S(1)} %get-tuple-element.32.decayed, f32[1024,128]{1,0:T(8,128)S(1)} %bitcast.4, ...), custom_call_target="tpu_custom_call" | custom-call | flops 1000000000 | bytes 4000000 | tf_op jit(solution)/shard_map/own_final/pallas_call | solution.py:392
  46.1 0.0 collective-permute-done.1
  46.1 1.2 %rest_final.1 = bf16[512,2048]{1,0:T(8,128)(2,1)} custom-call(s32[1]{0:T(128)} %bitcast.core_ref.refs_0_, bf16[512,1024]{1,0:T(8,128)(2,1)S(1)} %get-tuple-element.41.local, bf16[512,1024]{1,0:T(8,128)(2,1)S(1)} %get-tuple-element.42.decayed, f32[1024,128]{1,0:T(8,128)S(1)} %bitcast.3, ...), custom_call_target="tpu_custom_call", output_to_operand_aliasing={{}: (4, {})} | custom-call | flops 1000000000 | bytes 4000000 | tf_op jit(solution)/shard_map/rest_final/pallas_call | solution.py:415
Async XLA Ops:
  3.4 3.7 %collective-permute-start = (f32[16,72,128]{2,1,0:T(8,128)S(1)}, f32[16,72,128]{2,1,0:T(8,128)S(1)}, u32[]{:S(2)}, u32[]{:S(2)}) collective-permute-start(f32[16,72,128]{2,1,0:T(8,128)S(1)} %get-tuple-element.28), channel_id=1, source_target_pairs={{0,4},{4,0},{8,12},{12,8},{16,20},{20,16},{24,28},{28,24},{32,36},... | collective-permute-start | bytes 1769480 | tf_op jit(solution)/shard_map/ppermute | solution.py:439
  27.8 14.0 %all-to-all-start.1 = ((f32[16,64,128]{2,1,0:T(8,128)}), f32[16,64,128]{2,1,0:T(8,128)S(1)}, u32[]{:S(2)}, u32[]{:S(2)}) async-start(f32[16,64,128]{2,1,0:T(8,128)} %get-tuple-element.33), calls=%async_computation.1 | async-start | bytes 1048576 | tf_op jit(solution)/shard_map/all_to_all | solution.py:436
  42.0 4.1 %collective-permute-start.1 = (f32[16,64,128]{2,1,0:T(8,128)S(1)}, f32[16,64,128]{2,1,0:T(8,128)S(1)}, u32[]{:S(2)}, u32[]{:S(2)}) collective-permute-start(f32[16,64,128]{2,1,0:T(8,128)S(1)} %get-tuple-element.43), channel_id=1, source_target_pairs={{0,4},{4,0},{8,12},{12,8},{16,20},{20,16},{24,28},{28,24},{32,36},... | collective-permute-start | bytes 1572872 | tf_op jit(solution)/shard_map/ppermute | solution.py:447

commit v3 on v2

--- a/solution.py
+++ b/solution.py
@@ -20,7 +20,9 @@
 EARLY = 2
 WIDE = 512
 LOCAL_STEPS = WIDTH // WIDE
-CHUNKS = 4
+CHUNK = 1
+IN_FIRST = 10
+OUT_FIRST = 14
 ROWS = 64
 SLICE = ROWS + 8
 LOG2E = math.log2(math.e)
@@ -200,10 +202,12 @@
 
 def advance_kernel(core_ref, entry_ref, keep_ref, mine_ref, sent_ref):
     first = core_ref[0] == 0
-    entry = entry_ref[...]
-    advanced = entry * jnp.exp2(keep_ref[:, ROWS : ROWS + 1, :]) + keep_ref[:, 0:ROWS, :]
-    mine_ref[...] = jnp.where(first, entry, advanced)
-    sent_ref[...] = jnp.where(first, advanced, entry)
+    chips = entry_ref.shape[0]
+    for at in range(chips):
+        entry = entry_ref[(at + IN_FIRST - OUT_FIRST) % chips]
+        advanced = entry * jnp.exp2(keep_ref[at, ROWS : ROWS + 1, :]) + keep_ref[at, 0:ROWS, :]
+        mine_ref[at] = jnp.where(first, entry, advanced)
+        sent_ref[at] = jnp.where(first, advanced, entry)
 
 
 def advance(core, entry, keep):
@@ -223,14 +227,15 @@
     chips = in_ref.shape[0]
     copies = []
     for chip in range(chips):
-        out_ref[chip] = running
-        if (chip + 1) % CHUNKS == 0:
-            at = pl.ds(chip + 1 - CHUNKS, CHUNKS)
+        out_ref[(chip - OUT_FIRST) % chips] = running
+        if chip % CHUNK == CHUNK - 1:
+            at = pl.ds((chip + 1 - CHUNK - OUT_FIRST) % chips, CHUNK)
             copies.append(pltpu.make_async_copy(out_ref.at[at], out_hbm.at[at], sems.at[len(copies)]))
             copies[-1].start()
         if chip < chips - 1:
-            decay = jnp.exp2(in_ref[chip, ROWS : ROWS + 1, :])
-            running = running * decay + in_ref[chip, 0:ROWS, :]
+            place = (chip - IN_FIRST) % chips
+            decay = jnp.exp2(in_ref[place, ROWS : ROWS + 1, :])
+            running = running * decay + in_ref[place, 0:ROWS, :]
     wait_all(copies)
 
 
@@ -241,7 +246,7 @@
         in_specs=[VMEM],
         out_specs=[HBM, VMEM],
         out_shape=[pltpu.HBM(shape, jnp.float32), jax.ShapeDtypeStruct((8, DK), jnp.float32)],
-        scratch_shapes=[pltpu.VMEM(shape, jnp.float32), pltpu.SemaphoreType.DMA((shape[0] // CHUNKS,))],
+        scratch_shapes=[pltpu.VMEM(shape, jnp.float32), pltpu.SemaphoreType.DMA((shape[0] // CHUNK,))],
         compiler_params=pltpu.CompilerParams(vmem_limit_bytes=4 << 20),
         name="prefix",
     )(in_vmem(received))
@@ -307,7 +312,7 @@
     core = core_ref[0]
     steps = range(LOCAL_STEPS)
     queue = []
-    for i, half in ((0, core), (1, 1 - core)):
+    for i, half in ((0, 1 - core), (1, core)):
         targets = tuple(x.at[i] for x in (gate, key, query, value))
         queue += column_copies(half, steps, (gate_hbm, key_hbm, query_hbm, value_hbm), targets, sems.at[i], WIDE)
     early = pltpu.make_async_copy(gate_hbm.at[0:8, 0:DK], first, first_sem)
@@ -323,8 +328,8 @@
         stores[-1].start()
 
     for i, out, decayed, stored in (
-        (0, own_local, own_decayed, lambda which, cols: None),
-        (1, rest_local, rest_decayed, store),
+        (0, rest_local, rest_decayed, store),
+        (1, own_local, own_decayed, lambda which, cols: None),
     ):
         inputs = [x.at[i] for x in (query, key, value, gate)]
         for step in steps:
@@ -430,17 +435,17 @@
     chips = devices // 2
     core = lax.rem(lax.axis_index("seq"), 2).astype(jnp.int32)[None]
     swap = [(i, i ^ 1) for i in range(devices)]
-    same_core = [[2 * chip + c for chip in range(chips)] for c in range(2)]
-
-    def exchange(blocks):
+
+    def exchange(blocks, first):
+        same_core = [[2 * ((place + first) % chips) + c for place in range(chips)] for c in range(2)]
         return lax.all_to_all(blocks, "seq", split_axis=0, concat_axis=0, axis_index_groups=same_core, tiled=True)
 
     rest, *early = rest_states(core, log_gate, keys, values)
     own_other = lax.ppermute(rest, "seq", swap)
     own = own_states(core, log_gate, keys, values, early)
     combined, keep = combine(core, own, own_other)
-    entries, after = prefix(exchange(combined))
-    entry = exchange(entries)
+    entries, after = prefix(exchange(combined, IN_FIRST))
+    entry = exchange(entries, OUT_FIRST)
     own_local, own_decayed, rest_local, rest_decayed, after = local_part(core, queries, keys, values, log_gate, after)
     entry, after = lax.optimization_barrier((entry, after))
     own_entry, sent = advance(core, entry, keep)

time: 47.7 us -> 45.3 us (0.950)
  starting transfers between devices: 7.19 us -> 9.7 us
  blocking collectives: 19.7 us -> 17.4 us
  waiting for transfers between devices: 2.51 us -> 0.74 us
  Pallas kernels: 17.8 us -> 17 us
    all_to_all x1, starting transfers between devices: 3.59 us -> 7.17 us  [exchange(): lax.all_to_all(blocks, 'seq', split_axis=0, concat_axis=0, axis_index_gro...]
    all_to_all x1, blocking collectives: 19.7 us -> 17.4 us  [exchange(): lax.all_to_all(blocks, 'seq', split_axis=0, concat_axis=0, axis_index_gro...]
    all_to_all x1, waiting for transfers between devices: 2.51 us -> 0.73 us  [exchange(): lax.all_to_all(blocks, 'seq', split_axis=0, concat_axis=0, axis_index_gro...]
    ppermute x1, starting transfers between devices: 2.1 us -> 1.03 us  [on_device(): rest_entry = lax.ppermute(sent, 'seq', swap).reshape(HALF * DV, DK)]
    pallas_call x1, Pallas kernels: 7.91 us -> 7.09 us  [local_part(): pl.pallas_call(local_kernel, in_specs=[SMEM] + [HBM] * 4 + [ANY], out_spe...]
  transfers between devices with their start and end apart: 3 -> 3, of which waited for: 1 -> 1; matrix products, arithmetic and copies ran while one was open for 0% -> 0% of each run, Pallas kernels for 26% -> 25%
where the time goes in v3:
time: 45.3 us; the launch traced here: 45 us
  blocking collectives  17.4 us (38%)
  Pallas kernels  17 us (38%)
  starting transfers between devices  9.7 us (21%)
  waiting for transfers between devices  0.74 us (2%)
    all_to_all x1, blocking collectives, exchange(): lax.all_to_all(blocks, 'seq', split_axis=0, concat_axis=0, axis_index_gro...  17.4 us
    all_to_all x1, starting transfers between devices, exchange(): lax.all_to_all(blocks, 'seq', split_axis=0, concat_axis=0, axis_index_gro...  7.17 us
    pallas_call x1, Pallas kernels, local_part(): pl.pallas_call(local_kernel, in_specs=[SMEM] + [HBM] * 4 + [ANY], out_spe...  7.09 us
    pallas_call x1, Pallas kernels, rest_states(): pl.pallas_call(rest_states_kernel, in_specs=[SMEM, HBM, HBM, HBM], out_sp...  3.35 us
    pallas_call x1, Pallas kernels, own_states(): pl.pallas_call(own_states_kernel, in_specs=[SMEM, HBM, HBM, HBM] + [VMEM]...  2.2 us
    pallas_call x1, Pallas kernels, own_final(): pl.pallas_call(own_final_kernel, in_specs=[SMEM] + [VMEM] * 3 + [HBM] * 2...  2.01 us
    ppermute x1, starting transfers between devices, on_device(): own_other = lax.ppermute(rest, 'seq', swap)  1.5 us
    pallas_call x1, Pallas kernels, rest_final(): pl.pallas_call(rest_final_kernel, in_specs=[SMEM] + [VMEM] * 3 + [ANY], o...  1.24 us
  transfers between devices with their start and end apart: 3, of which 1 were waited for; matrix products, arithmetic and copies ran while one was open for 0% of the time, Pallas kernels for 25%

profile of v3, /device:TPU:1, one launch (start us, length us, event | category | flops | bytes accessed | tf_op | source)
XLA Modules:
  0.0 45.0 jit_solution(11019639795044037164)
XLA Ops:
  0.0 3.4 %rest_states.1 = (f32[16,72,128]{2,1,0:T(8,128)S(1)}, f32[512,512]{1,0:T(8,128)S(1)}, bf16[512,512]{1,0:T(8,128)(2,1)S(1)}, bf16[512,512]{1,0:T(8,128)(2,1)S(1)}) custom-call(s32[1]{0:T(128)} %bitcast.core_ref.refs_0_, f32[512,2048]{1,0:T(8,128)} %refs_4_.1, bf16[512,2048]{1,0:T(8,128)(2,1)} %refs_2_.1, bf16[512,2048]{1,0:T(8,128)(2,1)} %refs_3_.1), custom_call_target="tpu_custom_call" | custom-call | flops 1000000000 | bytes 9000000 | tf_op jit(solution)/shard_map/rest_states/pallas_call | solution.py:133
  3.4 1.5 %collective-permute-start = (f32[16,72,128]{2,1,0:T(8,128)S(1)}, f32[16,72,128]{2,1,0:T(8,128)S(1)}, u32[]{:S(2)}, u32[]{:S(2)}) collective-permute-start(f32[16,72,128]{2,1,0:T(8,128)S(1)} %get-tuple-element.28), channel_id=1, source_target_pairs={{0,4},{4,0},{8,12},{12,8},{16,20},{20,16},{24,28},{28,24},{32,36},... | collective-permute-start | bytes 1769480 | tf_op jit(solution)/shard_map/ppermute | solution.py:444
  4.9 2.2 %own_states.1.mine_ref = f32[16,72,128]{2,1,0:T(8,128)S(1)} custom-call(s32[1]{0:T(128)} %bitcast.core_ref.refs_0_, f32[512,2048]{1,0:T(8,128)} %refs_4_.1, bf16[512,2048]{1,0:T(8,128)(2,1)} %refs_2_.1, bf16[512,2048]{1,0:T(8,128)(2,1)} %refs_3_.1, f32[512,512]{1,0:T(8,128)S(1)} %get-tuple-element.25.early_gate, ...), custom_call_target="tpu_custom_call" | custom-call | flops 1000000000 | bytes 5000000 | tf_op jit(solution)/shard_map/own_states/pallas_call | solution.py:165
  7.1 0.0 collective-permute-done.other_ref
  7.1 0.1 combine.1
  7.2 17.4 %all_to_all.10.in_ref = f32[16,72,128]{2,1,0:T(8,128)S(1)} all-to-all(f32[16,72,128]{2,1,0:T(8,128)S(1)} %get-tuple-element.29), channel_id=1, replica_groups={{80,88,96,104,112,120,0,8,16,24,32,40,48,56,64,72},{84,92,100,108,116,1..., dimensions={0} | all-to-all | bytes 1179648 | tf_op jit(solution)/shard_map/all_to_all | solution.py:441
  24.6 0.9 %prefix.1 = (f32[16,64,128]{2,1,0:T(8,128)}, f32[8,128]{1,0:T(8,128)S(1)}) custom-call(f32[16,72,128]{2,1,0:T(8,128)S(1)} %all_to_all.10.in_ref), custom_call_target="tpu_custom_call" | custom-call | tf_op jit(solution)/shard_map/prefix/pallas_call | solution.py:244
  25.5 7.2 %all-to-all-start.1 = ((f32[16,64,128]{2,1,0:T(8,128)}), f32[16,64,128]{2,1,0:T(8,128)S(1)}, u32[]{:S(2)}, u32[]{:S(2)}) async-start(f32[16,64,128]{2,1,0:T(8,128)} %get-tuple-element.33), calls=%async_computation.1 | async-start | bytes 1048576 | tf_op jit(solution)/shard_map/all_to_all | solution.py:441
  32.7 7.1 %local_part.1 = (bf16[512,1024]{1,0:T(8,128)(2,1)S(1)}, bf16[512,1024]{1,0:T(8,128)(2,1)S(1)}, bf16[512,1024]{1,0:T(8,128)(2,1)}, bf16[512,1024]{1,0:T(8,128)(2,1)}, f32[8,128]{1,0:T(8,128)S(1)}) custom-call(s32[1]{0:T(128)} %bitcast.core_ref.refs_0_, bf16[512,2048]{1,0:T(8,128)(2,1)} %refs_1_.1, bf16[512,2048]{1,0:T(8,128)(2,1)} %refs_2_.1, ...), custom_call_target="tpu_custom_call" | custom-call | flops 8000000000 | bytes 16000000 | tf_op jit(solution)/shard_map/local_part/pallas_call | solution.py:351
  39.8 0.7 %all-to-all-done.1.entry_ref = f32[16,64,128]{2,1,0:T(8,128)S(1)} async-done(((f32[16,64,128]{2,1,0:T(8,128)}), f32[16,64,128]{2,1,0:T(8,128)S(1)}, u32[]{:S(2)}, u32[]{:S(2)}) %all-to-all-start.1) | async-done | bytes 524320 | tf_op jit(solution)/shard_map/all_to_all | solution.py:441
  40.6 0.1 advance.1
  40.7 1.0 %collective-permute-start.1 = (f32[16,64,128]{2,1,0:T(8,128)S(1)}, f32[16,64,128]{2,1,0:T(8,128)S(1)}, u32[]{:S(2)}, u32[]{:S(2)}) collective-permute-start(f32[16,64,128]{2,1,0:T(8,128)S(1)} %get-tuple-element.43), channel_id=1, source_target_pairs={{0,4},{4,0},{8,12},{12,8},{16,20},{20,16},{24,28},{28,24},{32,36},... | collective-permute-start | bytes 1572872 | tf_op jit(solution)/shard_map/ppermute | solution.py:452
  41.7 2.0 %own_final.1 = (bf16[512,2048]{1,0:T(8,128)(2,1)}, bf16[512,1024]{1,0:T(8,128)(2,1)S(1)}, bf16[512,1024]{1,0:T(8,128)(2,1)S(1)}) custom-call(s32[1]{0:T(128)} %bitcast.core_ref.refs_0_, bf16[512,1024]{1,0:T(8,128)(2,1)S(1)} %get-tuple-element.31.local, bf16[512,1024]{1,0:T(8,128)(2,1)S(1)} %get-tuple-element.32.decayed, f32[1024,128]{1,0:T(8,128)S(1)} %bitcast.4, ...), custom_call_target="tpu_custom_call" | custom-call | flops 1000000000 | bytes 4000000 | tf_op jit(solution)/shard_map/own_final/pallas_call | solution.py:397
  43.7 0.0 collective-permute-done.1
  43.7 1.2 %rest_final.1 = bf16[512,2048]{1,0:T(8,128)(2,1)} custom-call(s32[1]{0:T(128)} %bitcast.core_ref.refs_0_, bf16[512,1024]{1,0:T(8,128)(2,1)S(1)} %get-tuple-element.41.local, bf16[512,1024]{1,0:T(8,128)(2,1)S(1)} %get-tuple-element.42.decayed, f32[1024,128]{1,0:T(8,128)S(1)} %bitcast.3, ...), custom_call_target="tpu_custom_call", output_to_operand_aliasing={{}: (4, {})} | custom-call | flops 1000000000 | bytes 4000000 | tf_op jit(solution)/shard_map/rest_final/pallas_call | solution.py:420
Async XLA Ops:
  3.4 3.7 %collective-permute-start = (f32[16,72,128]{2,1,0:T(8,128)S(1)}, f32[16,72,128]{2,1,0:T(8,128)S(1)}, u32[]{:S(2)}, u32[]{:S(2)}) collective-permute-start(f32[16,72,128]{2,1,0:T(8,128)S(1)} %get-tuple-element.28), channel_id=1, source_target_pairs={{0,4},{4,0},{8,12},{12,8},{16,20},{20,16},{24,28},{28,24},{32,36},... | collective-permute-start | bytes 1769480 | tf_op jit(solution)/shard_map/ppermute | solution.py:444
  25.5 15.0 %all-to-all-start.1 = ((f32[16,64,128]{2,1,0:T(8,128)}), f32[16,64,128]{2,1,0:T(8,128)S(1)}, u32[]{:S(2)}, u32[]{:S(2)}) async-start(f32[16,64,128]{2,1,0:T(8,128)} %get-tuple-element.33), calls=%async_computation.1 | async-start | bytes 1048576 | tf_op jit(solution)/shard_map/all_to_all | solution.py:441
  40.7 3.0 %collective-permute-start.1 = (f32[16,64,128]{2,1,0:T(8,128)S(1)}, f32[16,64,128]{2,1,0:T(8,128)S(1)}, u32[]{:S(2)}, u32[]{:S(2)}) collective-permute-start(f32[16,64,128]{2,1,0:T(8,128)S(1)} %get-tuple-element.43), channel_id=1, source_target_pairs={{0,4},{4,0},{8,12},{12,8},{16,20},{20,16},{24,28},{28,24},{32,36},... | collective-permute-start | bytes 1572872 | tf_op jit(solution)/shard_map/ppermute | solution.py:452

commit v4 on v3

--- a/solution.py
+++ b/solution.py
@@ -20,8 +20,8 @@
 EARLY = 2
 WIDE = 512
 LOCAL_STEPS = WIDTH // WIDE
-CHUNK = 1
-IN_FIRST = 10
+CHUNK = 2
+IN_FIRST = 14
 OUT_FIRST = 14
 ROWS = 64
 SLICE = ROWS + 8
@@ -118,10 +118,13 @@
     sources = (gate_hbm, key_hbm, value_hbm)
     mine = column_copies(1 - core_ref[0], range(STEPS), sources, (gate, key, value), sems)
     early = column_copies(core_ref[0], range(EARLY), sources, (own_gate, own_key, own_value), own_sems)
-    for copies in mine + early:
+    for copies in mine:
         start_all(copies)
     for step in range(STEPS):
         wait_all(mine[step])
+        if step == 0:
+            for copies in early:
+                start_all(copies)
         states_step(step, gate, key, value, out_ref)
     for copies in early:
         wait_all(copies)

time: 45.3 us -> 44.8 us (0.989)
  starting transfers between devices: 9.7 us -> 9.07 us
    all_to_all x1, starting transfers between devices: 7.17 us -> 6.52 us  [exchange(): lax.all_to_all(blocks, 'seq', split_axis=0, concat_axis=0, axis_index_gro...]
where the time goes in v4:
time: 44.8 us; the launch traced here: 44.4 us
  blocking collectives  17.7 us (40%)
  Pallas kernels  16.8 us (38%)
  starting transfers between devices  9.07 us (20%)
  waiting for transfers between devices  0.74 us (2%)
    all_to_all x1, blocking collectives, exchange(): lax.all_to_all(blocks, 'seq', split_axis=0, concat_axis=0, axis_index_gro...  17.7 us
    pallas_call x1, Pallas kernels, local_part(): pl.pallas_call(local_kernel, in_specs=[SMEM] + [HBM] * 4 + [ANY], out_spe...  7.09 us
    all_to_all x1, starting transfers between devices, exchange(): lax.all_to_all(blocks, 'seq', split_axis=0, concat_axis=0, axis_index_gro...  6.52 us
    pallas_call x1, Pallas kernels, rest_states(): pl.pallas_call(rest_states_kernel, in_specs=[SMEM, HBM, HBM, HBM], out_sp...  3.2 us
    pallas_call x1, Pallas kernels, own_states(): pl.pallas_call(own_states_kernel, in_specs=[SMEM, HBM, HBM, HBM] + [VMEM]...  2.2 us
    pallas_call x1, Pallas kernels, own_final(): pl.pallas_call(own_final_kernel, in_specs=[SMEM] + [VMEM] * 3 + [HBM] * 2...  2.01 us
    ppermute x1, starting transfers between devices, on_device(): own_other = lax.ppermute(rest, 'seq', swap)  1.5 us
    pallas_call x1, Pallas kernels, rest_final(): pl.pallas_call(rest_final_kernel, in_specs=[SMEM] + [VMEM] * 3 + [ANY], o...  1.24 us
  transfers between devices with their start and end apart: 3, of which 1 were waited for; matrix products, arithmetic and copies ran while one was open for 0% of the time, Pallas kernels for 25%

profile of v4, /device:TPU:1, one launch (start us, length us, event | category | flops | bytes accessed | tf_op | source)
XLA Modules:
  0.0 44.4 jit_solution(7540464313742968089)
XLA Ops:
  0.0 3.2 %rest_states.1 = (f32[16,72,128]{2,1,0:T(8,128)S(1)}, f32[512,512]{1,0:T(8,128)S(1)}, bf16[512,512]{1,0:T(8,128)(2,1)S(1)}, bf16[512,512]{1,0:T(8,128)(2,1)S(1)}) custom-call(s32[1]{0:T(128)} %bitcast.core_ref.refs_0_, f32[512,2048]{1,0:T(8,128)} %refs_4_.1, bf16[512,2048]{1,0:T(8,128)(2,1)} %refs_2_.1, bf16[512,2048]{1,0:T(8,128)(2,1)} %refs_3_.1), custom_call_target="tpu_custom_call" | custom-call | flops 1000000000 | bytes 9000000 | tf_op jit(solution)/shard_map/rest_states/pallas_call | solution.py:136
  3.2 1.5 %collective-permute-start = (f32[16,72,128]{2,1,0:T(8,128)S(1)}, f32[16,72,128]{2,1,0:T(8,128)S(1)}, u32[]{:S(2)}, u32[]{:S(2)}) collective-permute-start(f32[16,72,128]{2,1,0:T(8,128)S(1)} %get-tuple-element.28), channel_id=1, source_target_pairs={{0,4},{4,0},{8,12},{12,8},{16,20},{20,16},{24,28},{28,24},{32,36},... | collective-permute-start | bytes 1769480 | tf_op jit(solution)/shard_map/ppermute | solution.py:447
  4.7 2.2 %own_states.1.mine_ref = f32[16,72,128]{2,1,0:T(8,128)S(1)} custom-call(s32[1]{0:T(128)} %bitcast.core_ref.refs_0_, f32[512,2048]{1,0:T(8,128)} %refs_4_.1, bf16[512,2048]{1,0:T(8,128)(2,1)} %refs_2_.1, bf16[512,2048]{1,0:T(8,128)(2,1)} %refs_3_.1, f32[512,512]{1,0:T(8,128)S(1)} %get-tuple-element.25.early_gate, ...), custom_call_target="tpu_custom_call" | custom-call | flops 1000000000 | bytes 5000000 | tf_op jit(solution)/shard_map/own_states/pallas_call | solution.py:168
  6.9 0.0 collective-permute-done.other_ref
  6.9 0.1 combine.1
  7.1 17.7 %all_to_all.10.in_ref = f32[16,72,128]{2,1,0:T(8,128)S(1)} all-to-all(f32[16,72,128]{2,1,0:T(8,128)S(1)} %get-tuple-element.29), channel_id=1, replica_groups={{112,120,0,8,16,24,32,40,48,56,64,72,80,88,96,104},{116,124,4,12,20,28,..., dimensions={0} | all-to-all | bytes 1179648 | tf_op jit(solution)/shard_map/all_to_all | solution.py:444
  24.8 0.9 %prefix.1 = (f32[16,64,128]{2,1,0:T(8,128)}, f32[8,128]{1,0:T(8,128)S(1)}) custom-call(f32[16,72,128]{2,1,0:T(8,128)S(1)} %all_to_all.10.in_ref), custom_call_target="tpu_custom_call" | custom-call | tf_op jit(solution)/shard_map/prefix/pallas_call | solution.py:247
  25.7 6.5 %all-to-all-start.1 = ((f32[16,64,128]{2,1,0:T(8,128)}), f32[16,64,128]{2,1,0:T(8,128)S(1)}, u32[]{:S(2)}, u32[]{:S(2)}) async-start(f32[16,64,128]{2,1,0:T(8,128)} %get-tuple-element.33), calls=%async_computation.1 | async-start | bytes 1048576 | tf_op jit(solution)/shard_map/all_to_all | solution.py:444
  32.2 7.1 %local_part.1 = (bf16[512,1024]{1,0:T(8,128)(2,1)S(1)}, bf16[512,1024]{1,0:T(8,128)(2,1)S(1)}, bf16[512,1024]{1,0:T(8,128)(2,1)}, bf16[512,1024]{1,0:T(8,128)(2,1)}, f32[8,128]{1,0:T(8,128)S(1)}) custom-call(s32[1]{0:T(128)} %bitcast.core_ref.refs_0_, bf16[512,2048]{1,0:T(8,128)(2,1)} %refs_1_.1, bf16[512,2048]{1,0:T(8,128)(2,1)} %refs_2_.1, ...), custom_call_target="tpu_custom_call" | custom-call | flops 8000000000 | bytes 16000000 | tf_op jit(solution)/shard_map/local_part/pallas_call | solution.py:354
  39.3 0.7 %all-to-all-done.1.entry_ref = f32[16,64,128]{2,1,0:T(8,128)S(1)} async-done(((f32[16,64,128]{2,1,0:T(8,128)}), f32[16,64,128]{2,1,0:T(8,128)S(1)}, u32[]{:S(2)}, u32[]{:S(2)}) %all-to-all-start.1) | async-done | bytes 524320 | tf_op jit(solution)/shard_map/all_to_all | solution.py:444
  40.0 0.1 advance.1
  40.1 1.0 %collective-permute-start.1 = (f32[16,64,128]{2,1,0:T(8,128)S(1)}, f32[16,64,128]{2,1,0:T(8,128)S(1)}, u32[]{:S(2)}, u32[]{:S(2)}) collective-permute-start(f32[16,64,128]{2,1,0:T(8,128)S(1)} %get-tuple-element.43), channel_id=1, source_target_pairs={{0,4},{4,0},{8,12},{12,8},{16,20},{20,16},{24,28},{28,24},{32,36},... | collective-permute-start | bytes 1572872 | tf_op jit(solution)/shard_map/ppermute | solution.py:455
  41.2 2.0 %own_final.1 = (bf16[512,2048]{1,0:T(8,128)(2,1)}, bf16[512,1024]{1,0:T(8,128)(2,1)S(1)}, bf16[512,1024]{1,0:T(8,128)(2,1)S(1)}) custom-call(s32[1]{0:T(128)} %bitcast.core_ref.refs_0_, bf16[512,1024]{1,0:T(8,128)(2,1)S(1)} %get-tuple-element.31.local, bf16[512,1024]{1,0:T(8,128)(2,1)S(1)} %get-tuple-element.32.decayed, f32[1024,128]{1,0:T(8,128)S(1)} %bitcast.4, ...), custom_call_target="tpu_custom_call" | custom-call | flops 1000000000 | bytes 4000000 | tf_op jit(solution)/shard_map/own_final/pallas_call | solution.py:400
  43.2 0.0 collective-permute-done.1
  43.2 1.2 %rest_final.1 = bf16[512,2048]{1,0:T(8,128)(2,1)} custom-call(s32[1]{0:T(128)} %bitcast.core_ref.refs_0_, bf16[512,1024]{1,0:T(8,128)(2,1)S(1)} %get-tuple-element.41.local, bf16[512,1024]{1,0:T(8,128)(2,1)S(1)} %get-tuple-element.42.decayed, f32[1024,128]{1,0:T(8,128)S(1)} %bitcast.3, ...), custom_call_target="tpu_custom_call", output_to_operand_aliasing={{}: (4, {})} | custom-call | flops 1000000000 | bytes 4000000 | tf_op jit(solution)/shard_map/rest_final/pallas_call | solution.py:423
Async XLA Ops:
  3.2 3.7 %collective-permute-start = (f32[16,72,128]{2,1,0:T(8,128)S(1)}, f32[16,72,128]{2,1,0:T(8,128)S(1)}, u32[]{:S(2)}, u32[]{:S(2)}) collective-permute-start(f32[16,72,128]{2,1,0:T(8,128)S(1)} %get-tuple-element.28), channel_id=1, source_target_pairs={{0,4},{4,0},{8,12},{12,8},{16,20},{20,16},{24,28},{28,24},{32,36},... | collective-permute-start | bytes 1769480 | tf_op jit(solution)/shard_map/ppermute | solution.py:447
  25.7 14.4 %all-to-all-start.1 = ((f32[16,64,128]{2,1,0:T(8,128)}), f32[16,64,128]{2,1,0:T(8,128)S(1)}, u32[]{:S(2)}, u32[]{:S(2)}) async-start(f32[16,64,128]{2,1,0:T(8,128)} %get-tuple-element.33), calls=%async_computation.1 | async-start | bytes 1048576 | tf_op jit(solution)/shard_map/all_to_all | solution.py:444
  40.1 3.1 %collective-permute-start.1 = (f32[16,64,128]{2,1,0:T(8,128)S(1)}, f32[16,64,128]{2,1,0:T(8,128)S(1)}, u32[]{:S(2)}, u32[]{:S(2)}) collective-permute-start(f32[16,64,128]{2,1,0:T(8,128)S(1)} %get-tuple-element.43), channel_id=1, source_target_pairs={{0,4},{4,0},{8,12},{12,8},{16,20},{20,16},{24,28},{28,24},{32,36},... | collective-permute-start | bytes 1572872 | tf_op jit(solution)/shard_map/ppermute | solution.py:455

commit v5 on v4

--- a/solution.py
+++ b/solution.py
@@ -21,8 +21,7 @@
 WIDE = 512
 LOCAL_STEPS = WIDTH // WIDE
 CHUNK = 2
-IN_FIRST = 14
-OUT_FIRST = 14
+FIRST = (14, 6)
 ROWS = 64
 SLICE = ROWS + 8
 LOG2E = math.log2(math.e)
@@ -205,9 +204,8 @@
 
 def advance_kernel(core_ref, entry_ref, keep_ref, mine_ref, sent_ref):
     first = core_ref[0] == 0
-    chips = entry_ref.shape[0]
-    for at in range(chips):
-        entry = entry_ref[(at + IN_FIRST - OUT_FIRST) % chips]
+    for at in range(entry_ref.shape[0]):
+        entry = entry_ref[at]
         advanced = entry * jnp.exp2(keep_ref[at, ROWS : ROWS + 1, :]) + keep_ref[at, 0:ROWS, :]
         mine_ref[at] = jnp.where(first, entry, advanced)
         sent_ref[at] = jnp.where(first, advanced, entry)
@@ -224,35 +222,36 @@
     )(core, in_vmem(entry), in_vmem(keep))
 
 
-def prefix_kernel(in_ref, out_hbm, done_ref, out_ref, sems):
+def prefix_kernel(core_ref, in_ref, out_hbm, done_ref, out_ref, sems):
     done_ref[...] = jnp.zeros_like(done_ref)
     running = jnp.zeros((ROWS, DK), jnp.float32)
     chips = in_ref.shape[0]
+    shift = jnp.where(core_ref[0] == 0, chips - FIRST[0], chips - FIRST[1])
     copies = []
     for chip in range(chips):
-        out_ref[(chip - OUT_FIRST) % chips] = running
+        place = lax.rem(chip + shift, chips)
+        out_ref[place] = running
         if chip % CHUNK == CHUNK - 1:
-            at = pl.ds((chip + 1 - CHUNK - OUT_FIRST) % chips, CHUNK)
+            at = pl.ds(place + 1 - CHUNK, CHUNK)
             copies.append(pltpu.make_async_copy(out_ref.at[at], out_hbm.at[at], sems.at[len(copies)]))
             copies[-1].start()
         if chip < chips - 1:
-            place = (chip - IN_FIRST) % chips
             decay = jnp.exp2(in_ref[place, ROWS : ROWS + 1, :])
             running = running * decay + in_ref[place, 0:ROWS, :]
     wait_all(copies)
 
 
-def prefix(received):
+def prefix(core, received):
     shape = (received.shape[0], ROWS, DK)
     return pl.pallas_call(
         prefix_kernel,
-        in_specs=[VMEM],
+        in_specs=[SMEM, VMEM],
         out_specs=[HBM, VMEM],
         out_shape=[pltpu.HBM(shape, jnp.float32), jax.ShapeDtypeStruct((8, DK), jnp.float32)],
         scratch_shapes=[pltpu.VMEM(shape, jnp.float32), pltpu.SemaphoreType.DMA((shape[0] // CHUNK,))],
         compiler_params=pltpu.CompilerParams(vmem_limit_bytes=4 << 20),
         name="prefix",
-    )(in_vmem(received))
+    )(core, in_vmem(received))
 
 
 def local_step(step, waits, query_ref, key_ref, value_ref, gate_ref, local_ref, decayed_ref, stored):
@@ -439,16 +438,16 @@
     core = lax.rem(lax.axis_index("seq"), 2).astype(jnp.int32)[None]
     swap = [(i, i ^ 1) for i in range(devices)]
 
-    def exchange(blocks, first):
-        same_core = [[2 * ((place + first) % chips) + c for place in range(chips)] for c in range(2)]
+    def exchange(blocks):
+        same_core = [[2 * ((place + FIRST[c]) % chips) + c for place in range(chips)] for c in range(2)]
         return lax.all_to_all(blocks, "seq", split_axis=0, concat_axis=0, axis_index_groups=same_core, tiled=True)
 
     rest, *early = rest_states(core, log_gate, keys, values)
     own_other = lax.ppermute(rest, "seq", swap)
     own = own_states(core, log_gate, keys, values, early)
     combined, keep = combine(core, own, own_other)
-    entries, after = prefix(exchange(combined, IN_FIRST))
-    entry = exchange(entries, OUT_FIRST)
+    entries, after = prefix(core, exchange(combined))
+    entry = exchange(entries)
     own_local, own_decayed, rest_local, rest_decayed, after = local_part(core, queries, keys, values, log_gate, after)
     entry, after = lax.optimization_barrier((entry, after))
     own_entry, sent = advance(core, entry, keep)

time: 44.8 us -> 44.7 us (level)
  starting transfers between devices: 9.07 us -> 7.22 us
  waiting for transfers between devices: 0.74 us -> 1.89 us
  blocking collectives: 17.7 us -> 18.2 us
    all_to_all x1, starting transfers between devices: 6.52 us -> 5.24 us  [exchange(): lax.all_to_all(blocks, 'seq', split_axis=0, concat_axis=0, axis_index_gro...]
    all_to_all x1, waiting for transfers between devices: 0.73 us -> 1.88 us  [exchange(): lax.all_to_all(blocks, 'seq', split_axis=0, concat_axis=0, axis_index_gro...]
    ppermute x1, starting transfers between devices: 1.04 us -> 0.47 us  [on_device(): rest_entry = lax.ppermute(sent, 'seq', swap).reshape(HALF * DV, DK)]
    all_to_all x1, blocking collectives: 17.7 us -> 18.2 us  [exchange(): lax.all_to_all(blocks, 'seq', split_axis=0, concat_axis=0, axis_index_gro...]
  transfers between devices with their start and end apart: 3 -> 3, of which waited for: 1 -> 1; matrix products, arithmetic and copies ran while one was open for 0% -> 0% of each run, Pallas kernels for 25% -> 26%
where the time goes in v5:
time: 44.7 us; the launch traced here: 44.3 us
  blocking collectives  18.2 us (41%)
  Pallas kernels  16.9 us (38%)
  starting transfers between devices  7.22 us (16%)
  waiting for transfers between devices  1.89 us (4%)
    all_to_all x1, blocking collectives, exchange(): lax.all_to_all(blocks, 'seq', split_axis=0, concat_axis=0, axis_index_gro...  18.2 us
    pallas_call x1, Pallas kernels, local_part(): pl.pallas_call(local_kernel, in_specs=[SMEM] + [HBM] * 4 + [ANY], out_spe...  7.09 us
    all_to_all x1, starting transfers between devices, exchange(): lax.all_to_all(blocks, 'seq', split_axis=0, concat_axis=0, axis_index_gro...  5.24 us
    pallas_call x1, Pallas kernels, rest_states(): pl.pallas_call(rest_states_kernel, in_specs=[SMEM, HBM, HBM, HBM], out_sp...  3.2 us
    pallas_call x1, Pallas kernels, own_states(): pl.pallas_call(own_states_kernel, in_specs=[SMEM, HBM, HBM, HBM] + [VMEM]...  2.2 us
    pallas_call x1, Pallas kernels, own_final(): pl.pallas_call(own_final_kernel, in_specs=[SMEM] + [VMEM] * 3 + [HBM] * 2...  2.01 us
    all_to_all x1, waiting for transfers between devices, exchange(): lax.all_to_all(blocks, 'seq', split_axis=0, concat_axis=0, axis_index_gro...  1.88 us
    ppermute x1, starting transfers between devices, on_device(): own_other = lax.ppermute(rest, 'seq', swap)  1.5 us
  transfers between devices with their start and end apart: 3, of which 1 were waited for; matrix products, arithmetic and copies ran while one was open for 0% of the time, Pallas kernels for 26%

profile of v5, /device:TPU:1, one launch (start us, length us, event | category | flops | bytes accessed | tf_op | source)
XLA Modules:
  0.0 44.3 jit_solution(12619616054669853649)
XLA Ops:
  0.0 3.2 %rest_states.1 = (f32[16,72,128]{2,1,0:T(8,128)S(1)}, f32[512,512]{1,0:T(8,128)S(1)}, bf16[512,512]{1,0:T(8,128)(2,1)S(1)}, bf16[512,512]{1,0:T(8,128)(2,1)S(1)}) custom-call(s32[1]{0:T(128)} %bitcast.core_ref.refs_0_, f32[512,2048]{1,0:T(8,128)} %refs_4_.1, bf16[512,2048]{1,0:T(8,128)(2,1)} %refs_2_.1, bf16[512,2048]{1,0:T(8,128)(2,1)} %refs_3_.1), custom_call_target="tpu_custom_call" | custom-call | flops 1000000000 | bytes 9000000 | tf_op jit(solution)/shard_map/rest_states/pallas_call | solution.py:135
  3.2 1.5 %collective-permute-start = (f32[16,72,128]{2,1,0:T(8,128)S(1)}, f32[16,72,128]{2,1,0:T(8,128)S(1)}, u32[]{:S(2)}, u32[]{:S(2)}) collective-permute-start(f32[16,72,128]{2,1,0:T(8,128)S(1)} %get-tuple-element.28), channel_id=1, source_target_pairs={{0,4},{4,0},{8,12},{12,8},{16,20},{20,16},{24,28},{28,24},{32,36},... | collective-permute-start | bytes 1769480 | tf_op jit(solution)/shard_map/ppermute | solution.py:446
  4.7 2.2 %own_states.1.mine_ref = f32[16,72,128]{2,1,0:T(8,128)S(1)} custom-call(s32[1]{0:T(128)} %bitcast.core_ref.refs_0_, f32[512,2048]{1,0:T(8,128)} %refs_4_.1, bf16[512,2048]{1,0:T(8,128)(2,1)} %refs_2_.1, bf16[512,2048]{1,0:T(8,128)(2,1)} %refs_3_.1, f32[512,512]{1,0:T(8,128)S(1)} %get-tuple-element.25.early_gate, ...), custom_call_target="tpu_custom_call" | custom-call | flops 1000000000 | bytes 5000000 | tf_op jit(solution)/shard_map/own_states/pallas_call | solution.py:167
  6.9 0.0 collective-permute-done.other_ref
  6.9 0.1 combine.1
  7.1 18.2 %all_to_all.10.in_ref = f32[16,72,128]{2,1,0:T(8,128)S(1)} all-to-all(f32[16,72,128]{2,1,0:T(8,128)S(1)} %get-tuple-element.29), channel_id=1, replica_groups={{112,120,0,8,16,24,32,40,48,56,64,72,80,88,96,104},{52,60,68,76,84,92,1..., dimensions={0} | all-to-all | bytes 1179648 | tf_op jit(solution)/shard_map/all_to_all | solution.py:443
  25.3 0.9 %prefix.1 = (f32[16,64,128]{2,1,0:T(8,128)}, f32[8,128]{1,0:T(8,128)S(1)}) custom-call(s32[1]{0:T(128)} %bitcast.core_ref.refs_0_, f32[16,72,128]{2,1,0:T(8,128)S(1)} %all_to_all.10.in_ref), custom_call_target="tpu_custom_call" | custom-call | tf_op jit(solution)/shard_map/prefix/pallas_call | solution.py:246
  26.2 5.2 %all-to-all-start.1 = ((f32[16,64,128]{2,1,0:T(8,128)}), f32[16,64,128]{2,1,0:T(8,128)S(1)}, u32[]{:S(2)}, u32[]{:S(2)}) async-start(f32[16,64,128]{2,1,0:T(8,128)} %get-tuple-element.33), calls=%async_computation.1 | async-start | bytes 1048576 | tf_op jit(solution)/shard_map/all_to_all | solution.py:443
  31.5 7.1 %local_part.1 = (bf16[512,1024]{1,0:T(8,128)(2,1)S(1)}, bf16[512,1024]{1,0:T(8,128)(2,1)S(1)}, bf16[512,1024]{1,0:T(8,128)(2,1)}, bf16[512,1024]{1,0:T(8,128)(2,1)}, f32[8,128]{1,0:T(8,128)S(1)}) custom-call(s32[1]{0:T(128)} %bitcast.core_ref.refs_0_, bf16[512,2048]{1,0:T(8,128)(2,1)} %refs_1_.1, bf16[512,2048]{1,0:T(8,128)(2,1)} %refs_2_.1, ...), custom_call_target="tpu_custom_call" | custom-call | flops 8000000000 | bytes 16000000 | tf_op jit(solution)/shard_map/local_part/pallas_call | solution.py:353
  38.6 1.9 %all-to-all-done.1.entry_ref = f32[16,64,128]{2,1,0:T(8,128)S(1)} async-done(((f32[16,64,128]{2,1,0:T(8,128)}), f32[16,64,128]{2,1,0:T(8,128)S(1)}, u32[]{:S(2)}, u32[]{:S(2)}) %all-to-all-start.1) | async-done | bytes 524320 | tf_op jit(solution)/shard_map/all_to_all | solution.py:443
  40.4 0.1 advance.1
  40.6 0.5 %collective-permute-start.1 = (f32[16,64,128]{2,1,0:T(8,128)S(1)}, f32[16,64,128]{2,1,0:T(8,128)S(1)}, u32[]{:S(2)}, u32[]{:S(2)}) collective-permute-start(f32[16,64,128]{2,1,0:T(8,128)S(1)} %get-tuple-element.43), channel_id=1, source_target_pairs={{0,4},{4,0},{8,12},{12,8},{16,20},{20,16},{24,28},{28,24},{32,36},... | collective-permute-start | bytes 1572872 | tf_op jit(solution)/shard_map/ppermute | solution.py:454
  41.0 2.0 %own_final.1 = (bf16[512,2048]{1,0:T(8,128)(2,1)}, bf16[512,1024]{1,0:T(8,128)(2,1)S(1)}, bf16[512,1024]{1,0:T(8,128)(2,1)S(1)}) custom-call(s32[1]{0:T(128)} %bitcast.core_ref.refs_0_, bf16[512,1024]{1,0:T(8,128)(2,1)S(1)} %get-tuple-element.31.local, bf16[512,1024]{1,0:T(8,128)(2,1)S(1)} %get-tuple-element.32.decayed, f32[1024,128]{1,0:T(8,128)S(1)} %bitcast.4, ...), custom_call_target="tpu_custom_call" | custom-call | flops 1000000000 | bytes 4000000 | tf_op jit(solution)/shard_map/own_final/pallas_call | solution.py:399
  43.0 0.0 collective-permute-done.1
  43.1 1.2 %rest_final.1 = bf16[512,2048]{1,0:T(8,128)(2,1)} custom-call(s32[1]{0:T(128)} %bitcast.core_ref.refs_0_, bf16[512,1024]{1,0:T(8,128)(2,1)S(1)} %get-tuple-element.41.local, bf16[512,1024]{1,0:T(8,128)(2,1)S(1)} %get-tuple-element.42.decayed, f32[1024,128]{1,0:T(8,128)S(1)} %bitcast.3, ...), custom_call_target="tpu_custom_call", output_to_operand_aliasing={{}: (4, {})} | custom-call | flops 1000000000 | bytes 4000000 | tf_op jit(solution)/shard_map/rest_final/pallas_call | solution.py:422
Async XLA Ops:
  3.2 3.7 %collective-permute-start = (f32[16,72,128]{2,1,0:T(8,128)S(1)}, f32[16,72,128]{2,1,0:T(8,128)S(1)}, u32[]{:S(2)}, u32[]{:S(2)}) collective-permute-start(f32[16,72,128]{2,1,0:T(8,128)S(1)} %get-tuple-element.28), channel_id=1, source_target_pairs={{0,4},{4,0},{8,12},{12,8},{16,20},{20,16},{24,28},{28,24},{32,36},... | collective-permute-start | bytes 1769480 | tf_op jit(solution)/shard_map/ppermute | solution.py:446
  26.2 14.2 %all-to-all-start.1 = ((f32[16,64,128]{2,1,0:T(8,128)}), f32[16,64,128]{2,1,0:T(8,128)S(1)}, u32[]{:S(2)}, u32[]{:S(2)}) async-start(f32[16,64,128]{2,1,0:T(8,128)} %get-tuple-element.33), calls=%async_computation.1 | async-start | bytes 1048576 | tf_op jit(solution)/shard_map/all_to_all | solution.py:443
  40.6 2.5 %collective-permute-start.1 = (f32[16,64,128]{2,1,0:T(8,128)S(1)}, f32[16,64,128]{2,1,0:T(8,128)S(1)}, u32[]{:S(2)}, u32[]{:S(2)}) collective-permute-start(f32[16,64,128]{2,1,0:T(8,128)S(1)} %get-tuple-element.43), channel_id=1, source_target_pairs={{0,4},{4,0},{8,12},{12,8},{16,20},{20,16},{24,28},{28,24},{32,36},... | collective-permute-start | bytes 1572872 | tf_op jit(solution)/shard_map/ppermute | solution.py:454

commit v6 on v5

--- a/solution.py
+++ b/solution.py
@@ -21,7 +21,7 @@
 WIDE = 512
 LOCAL_STEPS = WIDTH // WIDE
 CHUNK = 2
-FIRST = (14, 6)
+FIRST = (10, 6)
 ROWS = 64
 SLICE = ROWS + 8
 LOG2E = math.log2(math.e)

time: 44.7 us -> 45.4 us (1.016)
  starting transfers between devices: 7.22 us -> 8.18 us
    all_to_all x1, starting transfers between devices: 5.24 us -> 6.2 us  [exchange(): lax.all_to_all(blocks, 'seq', split_axis=0, concat_axis=0, axis_index_gro...]
  transfers between devices with their start and end apart: 3 -> 3, of which waited for: 1 -> 1; matrix products, arithmetic and copies ran while one was open for 0% -> 0% of each run, Pallas kernels for 26% -> 25%
where the time goes in v6:
time: 45.4 us; the launch traced here: 45 us
  blocking collectives  18 us (40%)
  Pallas kernels  16.9 us (37%)
  starting transfers between devices  8.18 us (18%)
  waiting for transfers between devices  1.96 us (4%)
    all_to_all x1, blocking collectives, exchange(): lax.all_to_all(blocks, 'seq', split_axis=0, concat_axis=0, axis_index_gro...  18 us
    pallas_call x1, Pallas kernels, local_part(): pl.pallas_call(local_kernel, in_specs=[SMEM] + [HBM] * 4 + [ANY], out_spe...  7.09 us
    all_to_all x1, starting transfers between devices, exchange(): lax.all_to_all(blocks, 'seq', split_axis=0, concat_axis=0, axis_index_gro...  6.2 us
    pallas_call x1, Pallas kernels, rest_states(): pl.pallas_call(rest_states_kernel, in_specs=[SMEM, HBM, HBM, HBM], out_sp...  3.2 us
    pallas_call x1, Pallas kernels, own_states(): pl.pallas_call(own_states_kernel, in_specs=[SMEM, HBM, HBM, HBM] + [VMEM]...  2.2 us
    pallas_call x1, Pallas kernels, own_final(): pl.pallas_call(own_final_kernel, in_specs=[SMEM] + [VMEM] * 3 + [HBM] * 2...  2.01 us
    all_to_all x1, waiting for transfers between devices, exchange(): lax.all_to_all(blocks, 'seq', split_axis=0, concat_axis=0, axis_index_gro...  1.96 us
    ppermute x1, starting transfers between devices, on_device(): own_other = lax.ppermute(rest, 'seq', swap)  1.5 us
  transfers between devices with their start and end apart: 3, of which 1 were waited for; matrix products, arithmetic and copies ran while one was open for 0% of the time, Pallas kernels for 25%

profile of v6, /device:TPU:1, one launch (start us, length us, event | category | flops | bytes accessed | tf_op | source)
XLA Modules:
  0.0 45.0 jit_solution(4213685465677139646)
XLA Ops:
  0.0 3.2 %rest_states.1 = (f32[16,72,128]{2,1,0:T(8,128)S(1)}, f32[512,512]{1,0:T(8,128)S(1)}, bf16[512,512]{1,0:T(8,128)(2,1)S(1)}, bf16[512,512]{1,0:T(8,128)(2,1)S(1)}) custom-call(s32[1]{0:T(128)} %bitcast.core_ref.refs_0_, f32[512,2048]{1,0:T(8,128)} %refs_4_.1, bf16[512,2048]{1,0:T(8,128)(2,1)} %refs_2_.1, bf16[512,2048]{1,0:T(8,128)(2,1)} %refs_3_.1), custom_call_target="tpu_custom_call" | custom-call | flops 1000000000 | bytes 9000000 | tf_op jit(solution)/shard_map/rest_states/pallas_call | solution.py:135
  3.2 1.5 %collective-permute-start = (f32[16,72,128]{2,1,0:T(8,128)S(1)}, f32[16,72,128]{2,1,0:T(8,128)S(1)}, u32[]{:S(2)}, u32[]{:S(2)}) collective-permute-start(f32[16,72,128]{2,1,0:T(8,128)S(1)} %get-tuple-element.28), channel_id=1, source_target_pairs={{0,4},{4,0},{8,12},{12,8},{16,20},{20,16},{24,28},{28,24},{32,36},... | collective-permute-start | bytes 1769480 | tf_op jit(solution)/shard_map/ppermute | solution.py:446
  4.7 2.2 %own_states.1.mine_ref = f32[16,72,128]{2,1,0:T(8,128)S(1)} custom-call(s32[1]{0:T(128)} %bitcast.core_ref.refs_0_, f32[512,2048]{1,0:T(8,128)} %refs_4_.1, bf16[512,2048]{1,0:T(8,128)(2,1)} %refs_2_.1, bf16[512,2048]{1,0:T(8,128)(2,1)} %refs_3_.1, f32[512,512]{1,0:T(8,128)S(1)} %get-tuple-element.25.early_gate, ...), custom_call_target="tpu_custom_call" | custom-call | flops 1000000000 | bytes 5000000 | tf_op jit(solution)/shard_map/own_states/pallas_call | solution.py:167
  6.9 0.0 collective-permute-done.other_ref
  6.9 0.1 combine.1
  7.1 18.0 %all_to_all.10.in_ref = f32[16,72,128]{2,1,0:T(8,128)S(1)} all-to-all(f32[16,72,128]{2,1,0:T(8,128)S(1)} %get-tuple-element.29), channel_id=1, replica_groups={{80,88,96,104,112,120,0,8,16,24,32,40,48,56,64,72},{52,60,68,76,84,92,1..., dimensions={0} | all-to-all | bytes 1179648 | tf_op jit(solution)/shard_map/all_to_all | solution.py:443
  25.0 0.9 %prefix.1 = (f32[16,64,128]{2,1,0:T(8,128)}, f32[8,128]{1,0:T(8,128)S(1)}) custom-call(s32[1]{0:T(128)} %bitcast.core_ref.refs_0_, f32[16,72,128]{2,1,0:T(8,128)S(1)} %all_to_all.10.in_ref), custom_call_target="tpu_custom_call" | custom-call | tf_op jit(solution)/shard_map/prefix/pallas_call | solution.py:246
  25.9 6.2 %all-to-all-start.1 = ((f32[16,64,128]{2,1,0:T(8,128)}), f32[16,64,128]{2,1,0:T(8,128)S(1)}, u32[]{:S(2)}, u32[]{:S(2)}) async-start(f32[16,64,128]{2,1,0:T(8,128)} %get-tuple-element.33), calls=%async_computation.1 | async-start | bytes 1048576 | tf_op jit(solution)/shard_map/all_to_all | solution.py:443
  32.1 7.1 %local_part.1 = (bf16[512,1024]{1,0:T(8,128)(2,1)S(1)}, bf16[512,1024]{1,0:T(8,128)(2,1)S(1)}, bf16[512,1024]{1,0:T(8,128)(2,1)}, bf16[512,1024]{1,0:T(8,128)(2,1)}, f32[8,128]{1,0:T(8,128)S(1)}) custom-call(s32[1]{0:T(128)} %bitcast.core_ref.refs_0_, bf16[512,2048]{1,0:T(8,128)(2,1)} %refs_1_.1, bf16[512,2048]{1,0:T(8,128)(2,1)} %refs_2_.1, ...), custom_call_target="tpu_custom_call" | custom-call | flops 8000000000 | bytes 16000000 | tf_op jit(solution)/shard_map/local_part/pallas_call | solution.py:353
  39.2 2.0 %all-to-all-done.1.entry_ref = f32[16,64,128]{2,1,0:T(8,128)S(1)} async-done(((f32[16,64,128]{2,1,0:T(8,128)}), f32[16,64,128]{2,1,0:T(8,128)S(1)}, u32[]{:S(2)}, u32[]{:S(2)}) %all-to-all-start.1) | async-done | bytes 524320 | tf_op jit(solution)/shard_map/all_to_all | solution.py:443
  41.2 0.1 advance.1
  41.3 0.5 %collective-permute-start.1 = (f32[16,64,128]{2,1,0:T(8,128)S(1)}, f32[16,64,128]{2,1,0:T(8,128)S(1)}, u32[]{:S(2)}, u32[]{:S(2)}) collective-permute-start(f32[16,64,128]{2,1,0:T(8,128)S(1)} %get-tuple-element.43), channel_id=1, source_target_pairs={{0,4},{4,0},{8,12},{12,8},{16,20},{20,16},{24,28},{28,24},{32,36},... | collective-permute-start | bytes 1572872 | tf_op jit(solution)/shard_map/ppermute | solution.py:454
  41.8 2.0 %own_final.1 = (bf16[512,2048]{1,0:T(8,128)(2,1)}, bf16[512,1024]{1,0:T(8,128)(2,1)S(1)}, bf16[512,1024]{1,0:T(8,128)(2,1)S(1)}) custom-call(s32[1]{0:T(128)} %bitcast.core_ref.refs_0_, bf16[512,1024]{1,0:T(8,128)(2,1)S(1)} %get-tuple-element.31.local, bf16[512,1024]{1,0:T(8,128)(2,1)S(1)} %get-tuple-element.32.decayed, f32[1024,128]{1,0:T(8,128)S(1)} %bitcast.4, ...), custom_call_target="tpu_custom_call" | custom-call | flops 1000000000 | bytes 4000000 | tf_op jit(solution)/shard_map/own_final/pallas_call | solution.py:399
  43.8 0.0 collective-permute-done.1
  43.8 1.2 %rest_final.1 = bf16[512,2048]{1,0:T(8,128)(2,1)} custom-call(s32[1]{0:T(128)} %bitcast.core_ref.refs_0_, bf16[512,1024]{1,0:T(8,128)(2,1)S(1)} %get-tuple-element.41.local, bf16[512,1024]{1,0:T(8,128)(2,1)S(1)} %get-tuple-element.42.decayed, f32[1024,128]{1,0:T(8,128)S(1)} %bitcast.3, ...), custom_call_target="tpu_custom_call", output_to_operand_aliasing={{}: (4, {})} | custom-call | flops 1000000000 | bytes 4000000 | tf_op jit(solution)/shard_map/rest_final/pallas_call | solution.py:422
Async XLA Ops:
  3.2 3.7 %collective-permute-start = (f32[16,72,128]{2,1,0:T(8,128)S(1)}, f32[16,72,128]{2,1,0:T(8,128)S(1)}, u32[]{:S(2)}, u32[]{:S(2)}) collective-permute-start(f32[16,72,128]{2,1,0:T(8,128)S(1)} %get-tuple-element.28), channel_id=1, source_target_pairs={{0,4},{4,0},{8,12},{12,8},{16,20},{20,16},{24,28},{28,24},{32,36},... | collective-permute-start | bytes 1769480 | tf_op jit(solution)/shard_map/ppermute | solution.py:446
  25.9 15.3 %all-to-all-start.1 = ((f32[16,64,128]{2,1,0:T(8,128)}), f32[16,64,128]{2,1,0:T(8,128)S(1)}, u32[]{:S(2)}, u32[]{:S(2)}) async-start(f32[16,64,128]{2,1,0:T(8,128)} %get-tuple-element.33), calls=%async_computation.1 | async-start | bytes 1048576 | tf_op jit(solution)/shard_map/all_to_all | solution.py:443
  41.3 2.5 %collective-permute-start.1 = (f32[16,64,128]{2,1,0:T(8,128)S(1)}, f32[16,64,128]{2,1,0:T(8,128)S(1)}, u32[]{:S(2)}, u32[]{:S(2)}) collective-permute-start(f32[16,64,128]{2,1,0:T(8,128)S(1)} %get-tuple-element.43), channel_id=1, source_target_pairs={{0,4},{4,0},{8,12},{12,8},{16,20},{20,16},{24,28},{28,24},{32,36},... | collective-permute-start | bytes 1572872 | tf_op jit(solution)/shard_map/ppermute | solution.py:454
